TPU v7x, 128 devices: a whole 4x4x4 slice. The times are simulated.
128 devices in a mesh: tm: 32 (over y, z, core), batch: 4 (over x).
Axes of the slice: x: 4, y: 4, z: 4, core: 2. Of those that a mesh axis runs over, the one named last changes fastest.
Arguments:
- frames: float32 [4, 64, 131072], P('batch', None, 'tm'), may hold values from -6 to 6
- clip_start: int32 [4, 131072], P('batch', 'tm'), may hold values from 0 to 131071, as said below
- code_ids: int32 [4, 65536], P('batch', 'tm'), may hold values from 0 to 2047
- cotangent: float32 [4, 64, 131072], P('batch', None, 'tm'), may hold values from -6 to 6
- enc_conv: float32 [4, 3, 64, 64], replicated, may hold values from -0.4375 to 0.4375
- enc_conv_bias: float32 [4, 64], replicated, may hold values from -2 to 2
- enc_proj: float32 [4, 64, 64], replicated, may hold values from -0.75 to 0.75
- enc_proj_bias: float32 [4, 64], replicated, may hold values from -2 to 2
- downscale_weight: float32 [4, 64, 64], replicated, may hold values from -0.375 to 0.375
- downscale_bias: float32 [64], replicated, may hold values from -2 to 2
- codebook: float32 [2048, 64], replicated, may hold values from -6 to 6
- up_weight: float32 [4, 64, 64], replicated, may hold values from -0.5 to 0.5
- up_bias: float32 [64], replicated, may hold values from -2 to 2
- dec_conv: float32 [4, 3, 64, 64], replicated, may hold values from -0.4375 to 0.4375
- dec_conv_bias: float32 [4, 64], replicated, may hold values from -2 to 2
- dec_proj: float32 [4, 64, 64], replicated, may hold values from -0.75 to 0.75
- dec_proj_bias: float32 [4, 64], replicated, may hold values from -2 to 2
Outputs:
- rebuilt: float32 [4, 64, 131072], P('batch', None, 'tm')
- frames_grad: float32 [4, 64, 131072], P('batch', None, 'tm')
- enc_conv_grad: float32 [4, 3, 64, 64], replicated
- enc_conv_bias_grad: float32 [4, 64], replicated
- enc_proj_grad: float32 [4, 64, 64], replicated
- enc_proj_bias_grad: float32 [4, 64], replicated
- down_grad: float32 [4, 64, 64], replicated
- down_bias_grad: float32 [64], replicated
- codebook_grad: float32 [2048, 64], replicated
- up_grad: float32 [4, 64, 64], replicated
- up_bias_grad: float32 [64], replicated
- dec_conv_grad: float32 [4, 3, 64, 64], replicated
- dec_conv_bias_grad: float32 [4, 64], replicated
- dec_proj_grad: float32 [4, 64, 64], replicated
- dec_proj_bias_grad: float32 [4, 64], replicated
Inputs may be any that keep to these rules, and one draw needn't show every extreme that they name: clip_start[w, t] is the first frame, within window w, of the clip that holds frame t: it is at most t and does not fall along t; the last frame of every window starts a clip of its own.
All inputs are finite; a program needn't handle non-finite values.
Results may differ from a plain program's by a relative error of at most 0.0003.
Values sent between devices are 32-bit elements; how exact they have to be, the bound alone decides.
No kernel may reach another device: no remote copies, remote signals or barrier semaphores. Data moves between devices by JAX's collectives and lax.ppermute only.
A program may use at most 256 MiB of HBM per device.

v0:
```python
import jax
import jax.numpy as jnp
from jax import lax
from jax.sharding import PartitionSpec as P

COMMIT = 0.02
MARGIN = 40
DILATIONS = (1, 3, 9, 27)


def with_halo(block, sides, width):
    for axis, dim in sides:
        count = lax.axis_size(axis)
        forward = [(i, i + 1) for i in range(count - 1)]
        backward = [(target, source) for source, target in forward]
        low = lax.ppermute(
            lax.slice_in_dim(block, block.shape[dim] - width, None, axis=dim), axis, forward
        )
        high = lax.ppermute(lax.slice_in_dim(block, 0, width, axis=dim), axis, backward)
        block = jnp.concatenate([low, block, high], axis=dim)
    return block


def matmul(weight, value_entries):
    return jnp.einsum("oi,wit->wot", weight, value_entries, precision=lax.Precision.HIGHEST)


def matmul_back(weight, value_entries):
    return jnp.einsum("oi,wot->wit", weight, value_entries, precision=lax.Precision.HIGHEST)


def outer_sum(left_rows, right_rows):
    return jnp.einsum("wot,wit->oi", left_rows, right_rows, precision=lax.Precision.HIGHEST)


def gelu_grad(value_entries, grad):
    return jax.vjp(jax.nn.gelu, value_entries)[1](grad)[0]


def fwd_rim(value_entries, depth):
    return with_halo(value_entries, (("tm", 2),), depth)


def back_rim(value_entries, depth):
    return with_halo(value_entries, (("tm", 2),), depth)


def tap_mask(clip_ext, start, span_len, offset):
    centre = lax.slice_in_dim(clip_ext, MARGIN + start, MARGIN + start + span_len, axis=1)
    other = lax.slice_in_dim(
        clip_ext, MARGIN + start + offset, MARGIN + start + offset + span_len, axis=1
    )
    return (centre == other).astype(jnp.float32)[:, None, :]


def pair_mask(clip_ext, first, second, length):
    left_ids = clip_ext[:, MARGIN + first : MARGIN + first + length : 2]
    right_ids = clip_ext[:, MARGIN + second : MARGIN + second + length : 2]
    return (left_ids == right_ids).astype(jnp.float32)[:, None, :]


def gather_pairs(padded, filter_weight, clip_ext, length):
    result = 0.0
    for k in range(4):
        tap_rows = padded[:, :, 1 + k : 1 + k + length : 2]
        result = result + matmul(filter_weight[k], tap_rows) * pair_mask(clip_ext, k - 1, 0, length)
    return result


def spread_pairs(padded, filter_weight, clip_ext, length):
    half_len = length // 2
    even_out = matmul(filter_weight[1], padded[:, :, 1 : half_len + 1]) + matmul(
        filter_weight[3], padded[:, :, 0:half_len]
    ) * pair_mask(clip_ext, 0, -2, length)
    odd_out = matmul(filter_weight[0], padded[:, :, 2 : half_len + 2]) * pair_mask(
        clip_ext, 1, 2, length
    ) + matmul(filter_weight[2], padded[:, :, 1 : half_len + 1]) * pair_mask(clip_ext, 1, 0, length)
    return jnp.stack([even_out, odd_out], axis=-1).reshape(
        even_out.shape[0], even_out.shape[1], length
    )


def stack_forward(value_entries, conv, conv_bias, proj, proj_bias, clip_ext, dilations):
    length = value_entries.shape[2]
    stored = []
    widened = with_halo(value_entries, (("tm", 2),), MARGIN)
    margin = MARGIN
    for section, dilation in enumerate(dilations):
        inner_rim = margin - dilation
        span_len = length + 2 * inner_rim
        active = jax.nn.gelu(widened)
        hidden = conv_bias[section][None, :, None]
        for k in range(3):
            hidden = hidden + matmul(
                conv[section, k], active[:, :, k * dilation : k * dilation + span_len]
            ) * tap_mask(clip_ext, -inner_rim, span_len, (k - 1) * dilation)
        gated_out = jax.nn.gelu(hidden)
        stored.append(
            (
                widened[:, :, margin : margin + length],
                active[:, :, margin - dilation : margin + length + dilation],
                hidden[:, :, inner_rim : inner_rim + length],
                gated_out[:, :, inner_rim : inner_rim + length],
            )
        )
        widened = (
            widened[:, :, dilation : dilation + span_len]
            + matmul(proj[section], gated_out)
            + proj_bias[section][None, :, None]
        )
        margin = inner_rim
    return (widened, stored)


def stack_backward(grad_out, stored, conv, proj, clip_ext, dilations):
    length = grad_out.shape[2]
    sections = len(dilations)
    conv_grads = [None] * sections
    conv_bias_grads = [None] * sections
    proj_grads = [None] * sections
    proj_bias_grads = [None] * sections
    for section in reversed(range(sections)):
        dilation = dilations[section]
        value_entries, active, hidden, gated_out = stored[section]
        proj_grads[section] = outer_sum(grad_out, gated_out)
        proj_bias_grads[section] = jnp.sum(grad_out, axis=(0, 2))
        hidden_grad = gelu_grad(hidden, matmul_back(proj[section], grad_out))
        conv_bias_grads[section] = jnp.sum(hidden_grad, axis=(0, 2))
        conv_grads[section] = jnp.stack(
            [
                outer_sum(
                    hidden_grad * tap_mask(clip_ext, 0, length, (k - 1) * dilation),
                    active[:, :, k * dilation : k * dilation + length],
                )
                for k in range(3)
            ]
        )
        padded = back_rim(hidden_grad, dilation)
        active_grad = 0.0
        for k in range(3):
            start = (2 - k) * dilation
            active_grad = active_grad + matmul_back(
                conv[section, k],
                padded[:, :, start : start + length]
                * tap_mask(clip_ext, 0, length, (1 - k) * dilation),
            )
        grad_out = grad_out + gelu_grad(value_entries, active_grad)
    return (
        grad_out,
        (
            jnp.stack(conv_grads),
            jnp.stack(conv_bias_grads),
            jnp.stack(proj_grads),
            jnp.stack(proj_bias_grads),
        ),
    )


def on_device(
    frames,
    clip_start,
    code_ids,
    cotangent,
    enc_conv,
    enc_conv_bias,
    enc_proj,
    enc_proj_bias,
    downscale_weight,
    downscale_bias,
    codebook,
    up_weight,
    up_bias,
    dec_conv,
    dec_conv_bias,
    dec_proj,
    dec_proj_bias,
):
    length = frames.shape[2]
    channels = frames.shape[1]
    backward_order = DILATIONS[::-1]
    clip_ext = with_halo(clip_start + 1, (("tm", 1),), MARGIN)
    encoder_output, enc_stored = stack_forward(
        frames, enc_conv, enc_conv_bias, enc_proj, enc_proj_bias, clip_ext, DILATIONS
    )
    enc_rim = fwd_rim(encoder_output, 2)
    latent = (
        gather_pairs(enc_rim, downscale_weight, clip_ext, length) + downscale_bias[None, :, None]
    )
    chosen = jnp.transpose(codebook[code_ids], (0, 2, 1))
    chosen_rim = fwd_rim(chosen, 1)
    upsampled = spread_pairs(chosen_rim, up_weight, clip_ext, length) + up_bias[None, :, None]
    rebuilt, dec_stored = stack_forward(
        upsampled, dec_conv, dec_conv_bias, dec_proj, dec_proj_bias, clip_ext, backward_order
    )
    up_grad_in, dec_grads = stack_backward(
        cotangent, dec_stored, dec_conv, dec_proj, clip_ext, backward_order
    )
    up_rim = back_rim(up_grad_in, 2)
    quant_grad = gather_pairs(up_rim, jnp.transpose(up_weight, (0, 2, 1)), clip_ext, length)
    up_grad = jnp.stack(
        [
            outer_sum(
                up_rim[:, :, 1 + k : 1 + k + length : 2] * pair_mask(clip_ext, k - 1, 0, length),
                chosen,
            )
            for k in range(4)
        ]
    )
    up_bias_grad = jnp.sum(up_grad_in, axis=(0, 2))
    latent_grad = quant_grad + 2.0 * COMMIT * (latent - chosen)
    code_terms = jnp.transpose(2.0 * (chosen - latent), (0, 2, 1)).reshape(-1, channels)
    codebook_grad = jax.ops.segment_sum(
        code_terms, code_ids.reshape(-1), num_segments=codebook.shape[0]
    )
    latent_rim = back_rim(latent_grad, 1)
    enc_grad_in = spread_pairs(
        latent_rim, jnp.transpose(downscale_weight, (0, 2, 1)), clip_ext, length
    )
    down_grad = jnp.stack(
        [
            outer_sum(
                latent_grad * pair_mask(clip_ext, k - 1, 0, length),
                enc_rim[:, :, 1 + k : 1 + k + length : 2],
            )
            for k in range(4)
        ]
    )
    down_bias_grad = jnp.sum(latent_grad, axis=(0, 2))
    frames_grad, enc_grads = stack_backward(
        enc_grad_in, enc_stored, enc_conv, enc_proj, clip_ext, DILATIONS
    )
    summed_all = lax.psum(
        (
            enc_grads[0],
            enc_grads[1],
            enc_grads[2],
            enc_grads[3],
            down_grad,
            down_bias_grad,
            dec_grads[0],
            dec_grads[1],
            dec_grads[2],
            dec_grads[3],
            up_grad,
            up_bias_grad,
            codebook_grad,
        ),
        ("tm", "batch"),
    )
    return (
        rebuilt,
        frames_grad,
        summed_all[0],
        summed_all[1],
        summed_all[2],
        summed_all[3],
        summed_all[4],
        summed_all[5],
        summed_all[12],
        summed_all[10],
        summed_all[11],
        summed_all[6],
        summed_all[7],
        summed_all[8],
        summed_all[9],
    )


def solution(mesh):
    return jax.shard_map(
        on_device,
        mesh=mesh,
        in_specs=(
            P("batch", None, "tm"),
            P("batch", "tm"),
            P("batch", "tm"),
            P("batch", None, "tm"),
            P(),
            P(),
            P(),
            P(),
            P(),
            P(),
            P(),
            P(),
            P(),
            P(),
            P(),
            P(),
            P(),
        ),
        out_specs=(
            P("batch", None, "tm"),
            P("batch", None, "tm"),
            P(),
            P(),
            P(),
            P(),
            P(),
            P(),
            P(),
            P(),
            P(),
            P(),
            P(),
            P(),
            P(),
        ),
        check_vma=False,
    )
```

profile of v0, /device:TPU:0, one launch (start us, length us, event | category | flops | bytes accessed | tf_op | source)
XLA Modules:
  0.0 697.0 jit_solution(16237123725478426927)
XLA Ops:
  9.3 3.0 collective-permute-start.1
  14.5 4.2 collective-permute-start.16
  20.8 5.5 gather_fusion
  26.7 3.8 collective-permute-start
  50.1 4.2 collective-permute-start.4
  70.2 2.6 fusion.160
  77.6 2.5 fusion.174
  87.9 17.7 %slice.1008 = f32[1,64,2048]{2,1,0:T(8,128)S(1)} slice(f32[1,64,4096]{2,1,0:T(8,128)S(1)} %fusion.63), slice={[0:1:1], [0:64:1], [0:4096:2]} | slice | bytes 1048576 | tf_op jit(solution)/shard_map/slice | solution.py:65
  106.9 4.3 collective-permute-start.18
  119.2 2.9 fusion.97
  124.5 3.4 fusion.104
  130.6 2.5 fusion.111
  137.6 2.6 fusion.125
  154.9 3.1 collective-permute-start.7
  163.9 2.6 fusion.806
  175.9 19.0 %slice.1012 = f32[1,64,2048]{2,1,0:T(8,128)} slice(f32[1,64,4100]{2,1,0:T(8,128)} %concatenate.189), slice={[0:1:1], [0:64:1], [4:4100:2]} | slice | bytes 1048576 | tf_op jit(solution)/shard_map/slice | solution.py:65
  194.9 18.4 %slice.1010 = f32[1,64,2048]{2,1,0:T(8,128)S(1)} slice(f32[1,64,4100]{2,1,0:T(8,128)} %concatenate.189), slice={[0:1:1], [0:64:1], [3:4099:2]} | slice | bytes 1048576 | tf_op jit(solution)/shard_map/slice | solution.py:65
  213.3 19.6 %slice.1006 = f32[1,64,2048]{2,1,0:T(8,128)} slice(f32[1,64,4100]{2,1,0:T(8,128)} %concatenate.189), slice={[0:1:1], [0:64:1], [1:4097:2]} | slice | bytes 1048576 | tf_op jit(solution)/shard_map/slice | solution.py:65
  232.9 3.4 convolution_bitcast_fusion.53
  238.6 3.6 collective-permute-start.9
  248.6 13.0 %scatter_custom_fusion = f32[2048,64]{1,0:T(8,128)} fusion(s32[2048]{0:T(1024)} %bitcast.1475, f32[2048,64]{1,0:T(8,128)} %copy.46, f32[]{:T(128)} %constant.80.clone.1), kind=kCustom, calls=%fused_computation.704 | custom fusion | flops 131072 | bytes 524800 | tf_op jit(solution)/shard_map/scatter-add | solution.py:212
  261.6 3.0 convolution_add_fusion.13
  264.8 3.4 fusion.807
  276.4 4.5 collective-permute-start.11
  283.1 3.1 collective-permute-done.10
  297.8 4.5 collective-permute-start.13
  305.3 3.5 collective-permute-done.12
  310.1 2.6 fusion.801
  313.5 17.6 %slice.947 = f32[1,64,2048]{2,1,0:T(8,128)S(1)} slice(f32[1,64,4096]{2,1,0:T(8,128)S(1)} %get-tuple-element.161), slice={[0:1:1], [0:64:1], [0:4096:2]} | slice | bytes 1048576 | tf_op jit(solution)/shard_map/slice | solution.py:65
  332.4 6.7 collective-permute-start.14
  343.6 17.6 %slice.951 = f32[1,64,2048]{2,1,0:T(8,128)S(1)} slice(f32[1,64,4100]{2,1,0:T(8,128)S(1)} %concatenate.187), slice={[0:1:1], [0:64:1], [4:4100:2]} | slice | bytes 1048576 | tf_op jit(solution)/shard_map/slice | solution.py:65
  363.8 18.1 %slice.949 = f32[1,64,2048]{2,1,0:T(8,128)} slice(f32[1,64,4100]{2,1,0:T(8,128)S(1)} %concatenate.187), slice={[0:1:1], [0:64:1], [3:4099:2]} | slice | bytes 1048576 | tf_op jit(solution)/shard_map/slice | solution.py:65
  382.0 17.8 %slice.944 = f32[1,64,2048]{2,1,0:T(8,128)S(1)} slice(f32[1,64,4100]{2,1,0:T(8,128)S(1)} %concatenate.187), slice={[0:1:1], [0:64:1], [1:4097:2]} | slice | bytes 1048576 | tf_op jit(solution)/shard_map/slice | solution.py:65
  403.0 2.6 fusion.800
  409.8 3.0 collective-permute-start.20
  420.5 4.3 copy.42
  424.8 5.2 convolution_bitcast_fusion.76
  430.0 3.1 fusion.791
  438.6 4.8 collective-permute-start.23
  444.9 3.1 copy.44
  448.0 2.7 collective-permute-done.22
  463.0 5.4 collective-permute-start.25
  470.0 3.0 collective-permute-done.24
  484.0 6.8 collective-permute-start.27
  506.4 8.7 %collective-permute-start.29 = (f32[1,64,1]{2,1,0:T(8,128)S(1)}, f32[1,64,1]{2,1,0:T(8,128)S(1)}, u32[]{:S(2)}, u32[]{:S(2)}) collective-permute-start(f32[1,64,1]{2,1,0:T(8,128)S(1)} %get-tuple-element.55), channel_id=1, source_target_pairs={{0,4},{4,8},{8,12},{12,16},{16,20},{20,24},{24,28},{28,32},{32,36}... | collective-permute-start | bytes 776 | tf_op jit(solution)/shard_map/ppermute | solution.py:16
  518.7 78.1 %all-reduce = (f32[4,64]{1,0:T(4,128)}, f32[4,64]{1,0:T(4,128)}, f32[64]{0:T(128)}, f32[64]{0:T(128)}, f32[4,64]{1,0:T(4,128)}, /*index=5*/f32[4,64]{1,0:T(4,128)}) all-reduce(f32[4,64]{1,0:T(4,128)S(1)} %get-tuple-element.180, f32[4,64]{1,0:T(4,128)S(1)} %get-tuple-element.181, ...), channel_id=1, replica_groups=mesh['tm'=32,'batch'=4] {'tm','batch'}, use_global_device_ids=true, to_apply=%region_5.0 | all-reduce | flops 1152 | bytes 9216 | tf_op jit(solution)/shard_map/psum | solution.py:232
  598.4 3.0 fusion.303
  601.3 81.8 %all-reduce.4.cloned.1.call-done = (f32[4,3,64,64]{3,2,1,0:T(8,128)}, f32[4,64,64]{2,1,0:T(8,128)}, f32[4,64,64]{2,1,0:T(8,128)}, f32[2048,64]{1,0:T(8,128)}, f3...) async-done(((f32[4,3,64,64]{3,2,1,0:T(8,128)}, f32[4,64,64]{2,1,0:T(8,128)}, f32[4,64,64]{2,1,0:T(8,128)}, f32[2048,64]{1,0:T(8,128)}, ...) | async-done | bytes 1179664 | tf_op jit(solution)/shard_map/psum | solution.py:232
  (509 shorter events, 220.0 us)
Async XLA Ops:
  7.2 676.0 %all-reduce.4.cloned.1.call-start = ((), (), s32[]{:S(2)}) async-start(), calls=%async_computation | async-start | bytes 4718592 | tf_op jit(solution)/shard_map/psum | solution.py:232
  8.0 25.4 %collective-permute-start.2 = (s32[1,40]{1,0:T(1,128)S(1)}, s32[1,40]{1,0:T(1,128)S(1)}, u32[]{:S(2)}, u32[]{:S(2)}) collective-permute-start(s32[1,40]{1,0:T(1,128)S(1)} %get-tuple-element.91), channel_id=1, source_target_pairs={{4,0},{8,4},{12,8},{16,12},{20,16},{24,20},{28,24},{32,28},{36,32}... | collective-permute-start | bytes 488 | tf_op jit(solution)/shard_map/ppermute | solution.py:19
  9.3 25.5 %collective-permute-start.1 = (s32[1,40]{1,0:T(1,128)S(1)}, s32[1,40]{1,0:T(1,128)S(1)}, u32[]{:S(2)}, u32[]{:S(2)}) collective-permute-start(s32[1,40]{1,0:T(1,128)S(1)} %get-tuple-element.92), channel_id=1, source_target_pairs={{0,4},{4,8},{8,12},{12,16},{16,20},{20,24},{24,28},{28,32},{32,36}... | collective-permute-start | bytes 488 | tf_op jit(solution)/shard_map/ppermute | solution.py:16
  13.2 44.5 %collective-permute-start.17 = (f32[1,64,40]{2,1,0:T(8,128)S(1)}, f32[1,64,40]{2,1,0:T(8,128)S(1)}, u32[]{:S(2)}, u32[]{:S(2)}) collective-permute-start(f32[1,64,40]{2,1,0:T(8,128)S(1)} %get-tuple-element.65), channel_id=1, source_target_pairs={{4,0},{8,4},{12,8},{16,12},{20,16},{24,20},{28,24},{32,28},{36,32}... | collective-permute-start | bytes 30728 | tf_op jit(solution)/shard_map/ppermute | solution.py:19
  14.5 43.2 %collective-permute-start.16 = (f32[1,64,40]{2,1,0:T(8,128)S(1)}, f32[1,64,40]{2,1,0:T(8,128)S(1)}, u32[]{:S(2)}, u32[]{:S(2)}) collective-permute-start(f32[1,64,40]{2,1,0:T(8,128)S(1)} %get-tuple-element.66), channel_id=1, source_target_pairs={{0,4},{4,8},{8,12},{12,16},{16,20},{20,24},{24,28},{28,32},{32,36}... | collective-permute-start | bytes 30728 | tf_op jit(solution)/shard_map/ppermute | solution.py:16
  26.7 15.8 %collective-permute-start = (f32[1,64,1]{2,1,0:T(8,128)S(1)}, f32[1,64,1]{2,1,0:T(8,128)S(1)}, u32[]{:S(2)}, u32[]{:S(2)}) collective-permute-start(f32[1,64,1]{2,1,0:T(8,128)S(1)} %get-tuple-element.81), channel_id=1, source_target_pairs={{0,4},{4,8},{8,12},{12,16},{16,20},{20,24},{24,28},{28,32},{32,36}... | collective-permute-start | bytes 776 | tf_op jit(solution)/shard_map/ppermute | solution.py:16
  33.5 8.3 %collective-permute-start.3 = (f32[1,64,1]{2,1,0:T(8,128)S(1)}, f32[1,64,1]{2,1,0:T(8,128)S(1)}, u32[]{:S(2)}, u32[]{:S(2)}) collective-permute-start(f32[1,64,1]{2,1,0:T(8,128)S(1)} %get-tuple-element.82), channel_id=1, source_target_pairs={{4,0},{8,4},{12,8},{16,12},{20,16},{24,20},{28,24},{32,28},{36,32}... | collective-permute-start | bytes 776 | tf_op jit(solution)/shard_map/ppermute | solution.py:19
  41.6 42.9 %copy-start.77 = (f32[1,4096]{1,0:T(1,128)}, f32[1,4096]{1,0:T(1,128)S(1)}, u32[]{:S(2)}) copy-start(f32[1,4096]{1,0:T(1,128)S(1)} %get-tuple-element.83) | copy-start | bytes 49156
  41.6 122.3 %copy-start.75 = (f32[1,4096]{1,0:T(1,128)}, f32[1,4096]{1,0:T(1,128)S(1)}, u32[]{:S(2)}) copy-start(f32[1,4096]{1,0:T(1,128)S(1)} %get-tuple-element.86) | copy-start | bytes 49156
  48.9 63.7 %collective-permute-start.5 = (f32[1,64,40]{2,1,0:T(8,128)}, f32[1,64,40]{2,1,0:T(8,128)}, u32[]{:S(2)}, u32[]{:S(2)}) collective-permute-start(f32[1,64,40]{2,1,0:T(8,128)} %get-tuple-element.77), channel_id=1, source_target_pairs={{4,0},{8,4},{12,8},{16,12},{20,16},{24,20},{28,24},{32,28},{36,32}... | collective-permute-start | bytes 30728 | tf_op jit(solution)/shard_map/ppermute | solution.py:19
  50.1 62.4 %collective-permute-start.4 = (f32[1,64,40]{2,1,0:T(8,128)}, f32[1,64,40]{2,1,0:T(8,128)}, u32[]{:S(2)}, u32[]{:S(2)}) collective-permute-start(f32[1,64,40]{2,1,0:T(8,128)} %get-tuple-element.78), channel_id=1, source_target_pairs={{0,4},{4,8},{8,12},{12,16},{16,20},{20,24},{24,28},{28,32},{32,36}... | collective-permute-start | bytes 30728 | tf_op jit(solution)/shard_map/ppermute | solution.py:16
  87.1 25.4 %copy-start.17 = (f32[1,64,4096]{2,1,0:T(8,128)}, f32[1,64,4096]{2,1,0:T(8,128)S(1)}, u32[]{:S(2)}) copy-start(f32[1,64,4096]{2,1,0:T(8,128)S(1)} %fusion.63) | copy-start | bytes 3145732
  87.2 24.0 %copy-start.68 = (f32[4,64,64]{2,1,0:T(8,128)S(1)}, f32[4,64,64]{2,1,0:T(8,128)}, u32[]{:S(2)}) copy-start(f32[4,64,64]{2,1,0:T(8,128)} %param.25) | copy-start | bytes 196612
  105.6 67.8 %collective-permute-start.19 = (f32[1,64,2]{2,1,0:T(8,128)}, f32[1,64,2]{2,1,0:T(8,128)}, u32[]{:S(2)}, u32[]{:S(2)}) collective-permute-start(f32[1,64,2]{2,1,0:T(8,128)} %get-tuple-element.63), channel_id=1, source_target_pairs={{4,0},{8,4},{12,8},{16,12},{20,16},{24,20},{28,24},{32,28},{36,32}... | collective-permute-start | bytes 1544 | tf_op jit(solution)/shard_map/ppermute | solution.py:19
  106.9 66.5 %collective-permute-start.18 = (f32[1,64,2]{2,1,0:T(8,128)}, f32[1,64,2]{2,1,0:T(8,128)}, u32[]{:S(2)}, u32[]{:S(2)}) collective-permute-start(f32[1,64,2]{2,1,0:T(8,128)} %get-tuple-element.64), channel_id=1, source_target_pairs={{0,4},{4,8},{8,12},{12,16},{16,20},{20,24},{24,28},{28,32},{32,36}... | collective-permute-start | bytes 1544 | tf_op jit(solution)/shard_map/ppermute | solution.py:16
  135.0 36.7 %copy-start.6 = (f32[1,64,4104]{2,1,0:T(8,128)}, f32[1,64,4104]{2,1,0:T(8,128)S(1)}, u32[]{:S(2)}) copy-start(f32[1,64,4104]{2,1,0:T(8,128)S(1)} %get-tuple-element.116) | copy-start | bytes 3151876
  154.9 9.0 %collective-permute-start.7 = (f32[1,64,1]{2,1,0:T(8,128)S(1)}, f32[1,64,1]{2,1,0:T(8,128)S(1)}, u32[]{:S(2)}, u32[]{:S(2)}) collective-permute-start(f32[1,64,1]{2,1,0:T(8,128)S(1)} %get-tuple-element.75), channel_id=1, source_target_pairs={{0,4},{4,8},{8,12},{12,16},{16,20},{20,24},{24,28},{28,32},{32,36}... | collective-permute-start | bytes 776 | tf_op jit(solution)/shard_map/ppermute | solution.py:16
  158.0 4.6 collective-permute-start.6
  213.3 31.0 %copy-start.22 = (f32[1,64,2048]{2,1,0:T(8,128)}, f32[1,64,2048]{2,1,0:T(8,128)S(1)}, u32[]{:S(2)}) copy-start(f32[1,64,2048]{2,1,0:T(8,128)S(1)} %slice.1010) | copy-start | bytes 1572868
  238.6 26.1 %collective-permute-start.9 = (f32[1,64,3]{2,1,0:T(8,128)}, f32[1,64,3]{2,1,0:T(8,128)}, u32[]{:S(2)}, u32[]{:S(2)}) collective-permute-start(f32[1,64,3]{2,1,0:T(8,128)} %get-tuple-element.73), channel_id=1, source_target_pairs={{0,4},{4,8},{8,12},{12,16},{16,20},{20,24},{24,28},{28,32},{32,36}... | collective-permute-start | bytes 2312 | tf_op jit(solution)/shard_map/ppermute | solution.py:16
  242.3 19.4 %collective-permute-start.8 = (f32[1,64,3]{2,1,0:T(8,128)}, f32[1,64,3]{2,1,0:T(8,128)}, u32[]{:S(2)}, u32[]{:S(2)}) collective-permute-start(f32[1,64,3]{2,1,0:T(8,128)} %get-tuple-element.74), channel_id=1, source_target_pairs={{4,0},{8,4},{12,8},{16,12},{20,16},{24,20},{28,24},{32,28},{36,32}... | collective-permute-start | bytes 2312 | tf_op jit(solution)/shard_map/ppermute | solution.py:19
  276.4 11.1 %collective-permute-start.11 = (f32[1,64,9]{2,1,0:T(8,128)S(1)}, f32[1,64,9]{2,1,0:T(8,128)S(1)}, u32[]{:S(2)}, u32[]{:S(2)}) collective-permute-start(f32[1,64,9]{2,1,0:T(8,128)S(1)} %get-tuple-element.71), channel_id=1, source_target_pairs={{0,4},{4,8},{8,12},{12,16},{16,20},{20,24},{24,28},{28,32},{32,36}... | collective-permute-start | bytes 6920 | tf_op jit(solution)/shard_map/ppermute | solution.py:16
  280.9 5.2 collective-permute-start.10
  296.1 8.6 %copy-start.114 = (f32[64]{0:T(128)S(1)}, f32[64]{0:T(128)}, u32[]{:S(2)}) copy-start(f32[64]{0:T(128)} %reduce_sum.198) | copy-start | bytes 772
  296.1 8.6 %copy-start.129 = (f32[64]{0:T(128)S(1)}, f32[64]{0:T(128)}, u32[]{:S(2)}) copy-start(f32[64]{0:T(128)} %get-tuple-element.162) | copy-start | bytes 772
  296.1 8.6 %copy-start.130 = (f32[64]{0:T(128)S(1)}, f32[64]{0:T(128)}, u32[]{:S(2)}) copy-start(f32[64]{0:T(128)} %get-tuple-element.170) | copy-start | bytes 772
  296.1 8.6 %copy-start.131 = (f32[64]{0:T(128)S(1)}, f32[64]{0:T(128)}, u32[]{:S(2)}) copy-start(f32[64]{0:T(128)} %get-tuple-element.164) | copy-start | bytes 772
  297.8 12.3 %collective-permute-start.13 = (f32[1,64,27]{2,1,0:T(8,128)S(1)}, f32[1,64,27]{2,1,0:T(8,128)S(1)}, u32[]{:S(2)}, u32[]{:S(2)}) collective-permute-start(f32[1,64,27]{2,1,0:T(8,128)S(1)} %get-tuple-element.69), channel_id=1, source_target_pairs={{0,4},{4,8},{8,12},{12,16},{16,20},{20,24},{24,28},{28,32},{32,36}... | collective-permute-start | bytes 20744 | tf_op jit(solution)/shard_map/ppermute | solution.py:16
  302.3 6.4 collective-permute-start.12
  312.7 27.6 %copy-start.41 = (f32[1,64,4096]{2,1,0:T(8,128)}, f32[1,64,4096]{2,1,0:T(8,128)S(1)}, u32[]{:S(2)}) copy-start(f32[1,64,4096]{2,1,0:T(8,128)S(1)} %get-tuple-element.161) | copy-start | bytes 3145732
  331.1 10.6 %collective-permute-start.15 = (f32[1,64,2]{2,1,0:T(8,128)}, f32[1,64,2]{2,1,0:T(8,128)S(1)}, u32[]{:S(2)}, u32[]{:S(2)}) collective-permute-start(f32[1,64,2]{2,1,0:T(8,128)} %get-tuple-element.67), channel_id=1, source_target_pairs={{4,0},{8,4},{12,8},{16,12},{20,16},{24,20},{28,24},{32,28},{36,32}... | collective-permute-start | bytes 1544 | tf_op jit(solution)/shard_map/ppermute | solution.py:19
  332.4 9.3 %collective-permute-start.14 = (f32[1,64,2]{2,1,0:T(8,128)}, f32[1,64,2]{2,1,0:T(8,128)}, u32[]{:S(2)}, u32[]{:S(2)}) collective-permute-start(f32[1,64,2]{2,1,0:T(8,128)} %get-tuple-element.68), channel_id=1, source_target_pairs={{0,4},{4,8},{8,12},{12,16},{16,20},{20,24},{24,28},{28,32},{32,36}... | collective-permute-start | bytes 1544 | tf_op jit(solution)/shard_map/ppermute | solution.py:16
  409.8 8.7 %collective-permute-start.20 = (f32[1,64,1]{2,1,0:T(8,128)S(1)}, f32[1,64,1]{2,1,0:T(8,128)S(1)}, u32[]{:S(2)}, u32[]{:S(2)}) collective-permute-start(f32[1,64,1]{2,1,0:T(8,128)S(1)} %get-tuple-element.79), channel_id=1, source_target_pairs={{0,4},{4,8},{8,12},{12,16},{16,20},{20,24},{24,28},{28,32},{32,36}... | collective-permute-start | bytes 776 | tf_op jit(solution)/shard_map/ppermute | solution.py:16
  412.9 4.8 collective-permute-start.21
  420.5 9.5 %copy-start.111 = (f32[4,64,64]{2,1,0:T(8,128)S(1)}, f32[4,64,64]{2,1,0:T(8,128)}, u32[]{:S(2)}) copy-start(f32[4,64,64]{2,1,0:T(8,128)} %param.23) | copy-start | bytes 196612
  438.6 14.7 %collective-permute-start.23 = (f32[1,64,27]{2,1,0:T(8,128)S(1)}, f32[1,64,27]{2,1,0:T(8,128)S(1)}, u32[]{:S(2)}, u32[]{:S(2)}) collective-permute-start(f32[1,64,27]{2,1,0:T(8,128)S(1)} %get-tuple-element.61), channel_id=1, source_target_pairs={{0,4},{4,8},{8,12},{12,16},{16,20},{20,24},{24,28},{28,32},{32,36}... | collective-permute-start | bytes 20744 | tf_op jit(solution)/shard_map/ppermute | solution.py:16
  443.4 7.4 %collective-permute-start.22 = (f32[1,64,27]{2,1,0:T(8,128)S(1)}, f32[1,64,27]{2,1,0:T(8,128)S(1)}, u32[]{:S(2)}, u32[]{:S(2)}) collective-permute-start(f32[1,64,27]{2,1,0:T(8,128)S(1)} %get-tuple-element.62), channel_id=1, source_target_pairs={{4,0},{8,4},{12,8},{16,12},{20,16},{24,20},{28,24},{32,28},{36,32}... | collective-permute-start | bytes 20744 | tf_op jit(solution)/shard_map/ppermute | solution.py:19
  463.0 11.3 %collective-permute-start.25 = (f32[1,64,9]{2,1,0:T(8,128)S(1)}, f32[1,64,9]{2,1,0:T(8,128)S(1)}, u32[]{:S(2)}, u32[]{:S(2)}) collective-permute-start(f32[1,64,9]{2,1,0:T(8,128)S(1)} %get-tuple-element.59), channel_id=1, source_target_pairs={{0,4},{4,8},{8,12},{12,16},{16,20},{20,24},{24,28},{28,32},{32,36}... | collective-permute-start | bytes 6920 | tf_op jit(solution)/shard_map/ppermute | solution.py:16
  468.4 4.5 collective-permute-start.24
  484.0 11.8 %collective-permute-start.27 = (f32[1,64,3]{2,1,0:T(8,128)S(1)}, f32[1,64,3]{2,1,0:T(8,128)S(1)}, u32[]{:S(2)}, u32[]{:S(2)}) collective-permute-start(f32[1,64,3]{2,1,0:T(8,128)S(1)} %get-tuple-element.57), channel_id=1, source_target_pairs={{0,4},{4,8},{8,12},{12,16},{16,20},{20,24},{24,28},{28,32},{32,36}... | collective-permute-start | bytes 2312 | tf_op jit(solution)/shard_map/ppermute | solution.py:16
  490.9 3.6 collective-permute-start.26
  505.2 11.8 %copy-start.71 = (f32[1,3,64,64]{3,2,1,0:T(8,128)S(1)}, f32[1,3,64,64]{3,2,1,0:T(8,128)}, u32[]{:S(2)}) copy-start(f32[1,3,64,64]{3,2,1,0:T(8,128)} %maximum_bitcast_fusion.7) | copy-start | bytes 147460
  505.2 11.8 %copy-start.72 = (f32[1,3,64,64]{3,2,1,0:T(8,128)S(1)}, f32[1,3,64,64]{3,2,1,0:T(8,128)}, u32[]{:S(2)}) copy-start(f32[1,3,64,64]{3,2,1,0:T(8,128)} %maximum_bitcast_fusion.6) | copy-start | bytes 147460
  505.2 11.8 %copy-start.73 = (f32[1,3,64,64]{3,2,1,0:T(8,128)S(1)}, f32[1,3,64,64]{3,2,1,0:T(8,128)}, u32[]{:S(2)}) copy-start(f32[1,3,64,64]{3,2,1,0:T(8,128)} %maximum_bitcast_fusion.5) | copy-start | bytes 147460
  505.3 11.8 %copy-start.74 = (f32[1,3,64,64]{3,2,1,0:T(8,128)S(1)}, f32[1,3,64,64]{3,2,1,0:T(8,128)}, u32[]{:S(2)}) copy-start(f32[1,3,64,64]{3,2,1,0:T(8,128)} %maximum_bitcast_fusion.4) | copy-start | bytes 147460
  506.4 91.8 %collective-permute-start.29 = (f32[1,64,1]{2,1,0:T(8,128)S(1)}, f32[1,64,1]{2,1,0:T(8,128)S(1)}, u32[]{:S(2)}, u32[]{:S(2)}) collective-permute-start(f32[1,64,1]{2,1,0:T(8,128)S(1)} %get-tuple-element.55), channel_id=1, source_target_pairs={{0,4},{4,8},{8,12},{12,16},{16,20},{20,24},{24,28},{28,32},{32,36}... | collective-permute-start | bytes 776 | tf_op jit(solution)/shard_map/ppermute | solution.py:16
  515.1 81.8 %collective-permute-start.28 = (f32[1,64,1]{2,1,0:T(8,128)S(1)}, f32[1,64,1]{2,1,0:T(8,128)S(1)}, u32[]{:S(2)}, u32[]{:S(2)}) collective-permute-start(f32[1,64,1]{2,1,0:T(8,128)S(1)} %get-tuple-element.56), channel_id=1, source_target_pairs={{4,0},{8,4},{12,8},{16,12},{20,16},{24,20},{28,24},{32,28},{36,32}... | collective-permute-start | bytes 776 | tf_op jit(solution)/shard_map/ppermute | solution.py:19
  518.0 78.8 %copy-start.40 = (f32[4096,64]{0,1:T(8,128)S(1)}, f32[4096,64]{0,1:T(8,128)}, u32[]{:S(2)}) copy-start(f32[4096,64]{0,1:T(8,128)} %fusion.385) | copy-start | bytes 3145732
  (125 other events, 367.8 us)
Sparse Core Ops, SparseCore 0:
  518.2 164.8 all-reduce.3
where the time goes:
time: 706 us; the launch traced here: 697 us
  local copies, waits for them, and re-layouts  198 us (28%)
  matrix products  184 us (26%)
  waiting for transfers between devices  98.2 us (14%)
  starting transfers between devices  91.5 us (13%)
  blocking collectives  78.1 us (11%)
  other arithmetic  30.3 us (4%)
  between operations  17.2 us (2%)
    slice x8, local copies, waits for them, and re-layouts, gather_pairs(): tap_rows = padded[:, :, 1 + k:1 + k + length:2]  146 us
    psum x1, waiting for transfers between devices, on_device(): lax.psum((enc_grads[0], enc_grads[1], enc_grads[2], enc_grads[3], down_gr...  81.8 us
    psum x1, blocking collectives, on_device(): lax.psum((enc_grads[0], enc_grads[1], enc_grads[2], enc_grads[3], down_gr...  78.1 us
    dot_general x48, matrix products, matmul(): jnp.einsum('oi,wit->wot', weight, value_entries, precision=lax.Precision....  71.4 us
    ppermute x15, starting transfers between devices, with_halo(): lax.ppermute(lax.slice_in_dim(block, block.shape[dim] - width, None, axis...  70.6 us
    dot_general x32, matrix products, matmul_back(): jnp.einsum('oi,wot->wit', weight, value_entries, precision=lax.Precision....  61.2 us
    dot_general x40, matrix products, outer_sum(): jnp.einsum('wot,wit->oi', left_rows, right_rows, precision=lax.Precision....  51.5 us
    ppermute x15, starting transfers between devices, with_halo(): lax.ppermute(lax.slice_in_dim(block, 0, width, axis=dim), axis, backward)  20.9 us
  transfers between devices with their start and end apart: 31, of which 7 were waited for; matrix products, arithmetic and copies ran while one was open for 25% of the time, Pallas kernels for 0%

commit v1 on v0

v1 whole, which is shorter than its diff:
```python
import functools

import jax
import jax.numpy as jnp
from jax import lax
from jax.experimental import pallas as pl
from jax.experimental.pallas import tpu as pltpu
from jax.sharding import PartitionSpec as P

COMMIT = 0.02
DILATIONS = (1, 3, 9, 27)
BF = jnp.bfloat16
F32 = jnp.float32
CH = 64
CODES = 2048
CORE = 4096
HALO = 128
EXT = CORE + 2 * HALO
HCORE = CORE // 2
HEXT = EXT // 2
STEP = 512
G0 = 0.7978845608028654
G1 = G0 * 0.044715
MB = 2**20
GRAD_PROJ = 384
GRAD_PAIR = 512
GRAD_BIAS = 640
GRAD_ROWS = 704


def dot(a, b):
    return jnp.dot(a, b, preferred_element_type=F32)


def dot_nt(a, b):
    return lax.dot_general(a, b, (((1,), (1,)), ((), ())), preferred_element_type=F32)


def split(v):
    hi = v.astype(BF)
    return hi, (v - hi.astype(F32)).astype(BF)


def gelu_both(v):
    s = v * v
    t = jnp.tanh(v * (G0 + G1 * s))
    cdf = 0.5 + 0.5 * t
    slope = cdf + (0.5 * v) * (1.0 - t * t) * (G0 + (3.0 * G1) * s)
    return v * cdf, slope


def tile_rows(rows, times):
    return jnp.concatenate([rows] * times, axis=0)


def aligned(start):
    return start if isinstance(start, int) else pl.multiple_of(start, 128)


def lanes(ref, start, size, rows=slice(None)):
    return ref[rows, pl.ds(aligned(start), size)]


def wrap(start, length):
    return start % length if isinstance(start, int) else lax.rem(start + length, length)


def from_left(ref, rows, start, size, offset, length):
    win = jnp.concatenate(
        [lanes(ref, wrap(start - 128, length), 128, rows), lanes(ref, start, size, rows)], axis=1
    )
    return pltpu.roll(win, offset, 1)[:, 128:]


def from_right(ref, rows, start, size, offset, length):
    win = jnp.concatenate(
        [lanes(ref, start, size, rows), lanes(ref, wrap(start + size, length), 128, rows)], axis=1
    )
    return pltpu.roll(win, size + 128 - offset, 1)[:, :size]


def sweep(fn, step=STEP):
    def body(i, carry):
        fn(i * step, step, True)
        return carry

    lax.fori_loop(0, CORE // step, body, 0)
    fn(CORE, 2 * HALO, False)


def half_sweep(fn, step=STEP // 2):
    def body(i, carry):
        fn(i * step, step, True)
        return carry

    lax.fori_loop(0, HCORE // step, body, 0)
    fn(HCORE, HALO, False)


def lane_fold(v):
    out = v[:, :128]
    for i in range(1, v.shape[1] // 128):
        out = out + v[:, i * 128 : (i + 1) * 128]
    return out


def selector():
    row = lax.broadcasted_iota(jnp.int32, (256, 256), 0)
    col = lax.broadcasted_iota(jnp.int32, (256, 256), 1)
    source = jnp.where(col < 128, 2 * col, 2 * (col - 128) + 1)
    return jnp.where(row == source, 1.0, 0.0).astype(BF)


def prep_kernel(
    ec, ecb, ep, epb, dw, db, cb, uw, ub, dc, dcb, dp, dpb,
    wf, wb, pf, pb, dg, ds_, ug, us, cbt, bias,
):
    def forms(w):
        hi, lo = split(w)
        return jnp.concatenate([hi, hi, lo], axis=1)

    def stacked(w):
        hi, lo = split(w)
        return jnp.concatenate([hi, lo], axis=0)

    def column(row):
        return jnp.broadcast_to(row, (128, CH)).T

    for n, (conv, cbias, proj, pbias) in enumerate(((ec, ecb, ep, epb), (dc, dcb, dp, dpb))):
        for b in range(4):
            at = 4 * n + b
            wf[at] = forms(conv[b].reshape(3 * CH, CH))
            wb[at] = stacked(jnp.concatenate([conv[b, k].T for k in range(3)], axis=1))
            pf[at] = forms(proj[b])
            pb[at] = forms(proj[b].T)
            bias[2 * at] = column(cbias[b : b + 1, :])
            bias[2 * at + 1] = column(pbias[b : b + 1, :])
    bias[16] = column(db[...])
    bias[17] = column(ub[...])
    dg[...] = stacked(jnp.concatenate([dw[k] for k in range(4)], axis=1))
    ds_[...] = forms(jnp.concatenate([dw[k].T for k in range(4)], axis=0))
    ug[...] = stacked(jnp.concatenate([uw[k].T for k in range(4)], axis=1))
    us[...] = forms(jnp.concatenate([uw[k] for k in range(4)], axis=0))
    cbt[...] = stacked(cb[...].T)


def stack_forward(x_ref, z_refs, blocks, dils, wf, pf, bias, mf, keep, last):
    def enter(value, start, size, b):
        act, slope = gelu_both(value)
        hi, lo = split(act)
        a_ref, gx_ref, _, _ = keep(b)
        a_ref[:CH, pl.ds(aligned(start), size)] = hi
        a_ref[CH:, pl.ds(aligned(start), size)] = lo
        gx_ref[:, pl.ds(aligned(start), size)] = slope
        z_refs[b % 2][:, pl.ds(aligned(start), size)] = dot(
            wf[blocks + b], jnp.concatenate([hi, lo, hi], axis=0)
        )

    def first(start, size, core):
        enter(lanes(x_ref, start, size), start, size, 0)

    sweep(first)
    for b in range(4):
        d = dils[b]
        m = DILATIONS.index(d)
        z_ref = z_refs[b % 2]

        def step(start, size, core, b=b, d=d, m=m, z_ref=z_ref):
            _, _, u_ref, gh_ref = keep(b)
            times = size // 128
            left = tile_rows(lanes(mf, start, size, slice(16 * m, 16 * m + 8)), 8)
            right = tile_rows(lanes(mf, start, size, slice(16 * m + 8, 16 * m + 16)), 8)
            cb = jnp.concatenate([bias[2 * (blocks + b)]] * times, axis=1)
            hidden = lanes(z_ref, start, size, slice(CH, 2 * CH)) + cb
            hidden = hidden + left * from_left(z_ref, slice(0, CH), start, size, d, EXT)
            hidden = hidden + right * from_right(z_ref, slice(2 * CH, 3 * CH), start, size, d, EXT)
            act, slope = gelu_both(hidden)
            hi, lo = split(act)
            u_ref[:CH, pl.ds(aligned(start), size)] = hi
            u_ref[CH:, pl.ds(aligned(start), size)] = lo
            gh_ref[:, pl.ds(aligned(start), size)] = slope
            pbias = jnp.concatenate([bias[2 * (blocks + b) + 1]] * times, axis=1)
            out = (
                lanes(x_ref, start, size)
                + dot(pf[blocks + b], jnp.concatenate([hi, lo, hi], axis=0))
                + pbias
            )
            if b < 3:
                x_ref[:, pl.ds(aligned(start), size)] = out
                enter(out, start, size, b + 1)
            else:
                last(out, start, size, core)

        sweep(step)


def stack_backward(g_ref, gh_refs, blocks, dils, wb, pb, mb, keep, acc, finish, last):
    dk1, dk2, dpa, csum, psum = acc

    def enter(grad, start, size, core, b):
        _, _, u_ref, slope_ref = keep(b)
        hi, lo = split(grad)
        q = dot(pb[blocks + b], jnp.concatenate([hi, lo, hi], axis=0))
        gh = lanes(slope_ref, start, size) * q
        ghi, glo = split(gh)
        gh_refs[b % 2][:CH, pl.ds(aligned(start), size)] = ghi
        gh_refs[b % 2][CH:, pl.ds(aligned(start), size)] = glo
        if core:
            dpa[b] += dot_nt(jnp.concatenate([hi, lo], axis=0), lanes(u_ref, start, size))
            csum[b] += lane_fold(gh)
            psum[b] += lane_fold(grad)

    for ref in acc:
        ref[...] = jnp.zeros(ref.shape, ref.dtype)

    def first(start, size, core):
        enter(lanes(g_ref, start, size), start, size, core, 3)

    sweep(first)
    for b in (3, 2, 1, 0):
        d = dils[b]
        m = DILATIONS.index(d)
        gh_ref = gh_refs[b % 2]

        def step(start, size, core, b=b, d=d, m=m, gh_ref=gh_ref):
            a_ref, gx_ref, _, _ = keep(b)
            left = tile_rows(lanes(mb, start, size, slice(32 * m, 32 * m + 16)), 4)
            right = tile_rows(lanes(mb, start, size, slice(32 * m + 16, 32 * m + 32)), 4)
            parts = []
            for rows in (slice(0, CH), slice(CH, 2 * CH)):
                parts.append(
                    jnp.concatenate(
                        [
                            from_right(gh_ref, rows, start, size, d, EXT) * right,
                            lanes(gh_ref, start, size, rows),
                            from_left(gh_ref, rows, start, size, d, EXT) * left,
                        ],
                        axis=0,
                    )
                )
            ghi, glo = parts
            both = dot(wb[blocks + b], ghi)
            ga = both[:CH] + both[CH:] + dot(wb[blocks + b, :CH], glo)
            if core:
                act = lanes(a_ref, start, size)
                dk1[b] += dot_nt(ghi, act)
                dk2[b] += dot_nt(glo, act[:CH])
            out = lanes(g_ref, start, size) + lanes(gx_ref, start, size) * ga
            if b > 0:
                g_ref[:, pl.ds(aligned(start), size)] = out
                enter(out, start, size, core, b - 1)
            else:
                last(out, start, size, core)

        sweep(step)
    for b in range(4):
        dk = dk1[b, :, :CH] + dk1[b, :, CH:] + dk2[b]
        dp = dpa[b, :CH, :CH] + dpa[b, CH:, :CH] + dpa[b, :CH, CH:]
        finish(b, dk, dp, csum[b], psum[b])


def store_grads(grads):
    kept = {}

    def finish(b, dk, dp, csum, psum):
        kept[b] = (dk, dp)
        if b % 2:
            at = b // 2
            grads[at * 192 : (at + 1) * 192, :] = jnp.concatenate([kept[b - 1][0], dk], axis=1)
            grads[GRAD_PROJ + at * CH : GRAD_PROJ + (at + 1) * CH, :] = jnp.concatenate(
                [kept[b - 1][1], dp], axis=1
            )
        put_column(grads, 2 * b, csum)
        put_column(grads, 2 * b + 1, psum)

    return finish


def put_column(grads, at, folded):
    lane = lax.broadcasted_iota(jnp.int32, (CH, 128), 1)
    total = jnp.sum(folded, axis=1, keepdims=True)
    grads[GRAD_BIAS:, :] = jnp.where(lane == at, total, grads[GRAD_BIAS:, :])


def to_halves(value, sel, e_ref, o_ref, start, size):
    hi, lo = split(value)
    both = jnp.concatenate([hi, lo], axis=0)
    half = start // 2
    for i in range(size // 256):
        out = dot(both[:, i * 256 : (i + 1) * 256], sel).astype(BF)
        e_ref[:, pl.ds(aligned(half + i * 128), 128)] = out[:, :128]
        o_ref[:, pl.ds(aligned(half + i * 128), 128)] = out[:, 128:]


def pair_stack(e_ref, o_ref, mhb, start, size):
    masks = [tile_rows(lanes(mhb, start, size, slice(16 * i, 16 * i + 16)), 4) for i in range(3)]
    parts = []
    for rows in (slice(0, CH), slice(CH, 2 * CH)):
        parts.append(
            jnp.concatenate(
                [
                    from_left(o_ref, rows, start, size, 1, HEXT) * masks[0],
                    lanes(e_ref, start, size, rows),
                    lanes(o_ref, start, size, rows) * masks[1],
                    from_right(e_ref, rows, start, size, 1, HEXT) * masks[2],
                ],
                axis=0,
            )
        )
    return parts


def pair_gather(w, parts):
    both = dot(w[...], parts[0])
    return both[:CH] + both[CH:] + dot(w[:CH], parts[1])


def spread(w, hl_ref, mh, z_ref, sel, bias_tile, x_ref):
    def first(start, size, core):
        both = lanes(hl_ref, start, size)
        z = dot(w[...], jnp.concatenate([both, both[:CH]], axis=0))
        masks = [tile_rows(lanes(mh, start, size, slice(8 * i, 8 * i + 8)), 8) for i in range(3)]
        at = pl.ds(aligned(start), size)
        z_ref[0:64, at] = z[0:64] * masks[0]
        z_ref[64:128, at] = z[64:128]
        z_ref[128:192, at] = z[128:192] * masks[1]
        z_ref[192:256, at] = z[192:256] * masks[2]

    half_sweep(first)

    def second(start, size, core):
        even = lanes(z_ref, start, size, slice(64, 128)) + from_left(
            z_ref, slice(192, 256), start, size, 1, HEXT
        )
        odd = lanes(z_ref, start, size, slice(128, 192)) + from_right(
            z_ref, slice(0, 64), start, size, 1, HEXT
        )
        ehi, elo = split(even)
        ohi, olo = split(odd)
        for i in range(size // 128):
            cut = slice(i * 128, (i + 1) * 128)
            rows = jnp.concatenate(
                [
                    jnp.concatenate([ehi[:, cut], ohi[:, cut]], axis=1),
                    jnp.concatenate([elo[:, cut], olo[:, cut]], axis=1),
                ],
                axis=0,
            )
            out = dot_nt(rows, sel)
            out = out[:CH] + out[CH:]
            if bias_tile is not None:
                out = out + jnp.concatenate([bias_tile, bias_tile], axis=1)
            x_ref[:, pl.ds(aligned(2 * start + 256 * i), 256)] = out

    half_sweep(second)


def one_hot(ids_row, first, count):
    row = lax.broadcasted_iota(jnp.int32, (count, ids_row.shape[1]), 0) + first
    return jnp.where(row == ids_row, 1.0, 0.0).astype(BF)


def encode_kernel(
    frames, lo, hi, clip, codes, wf, pf, dg, cbt, bias,
    mf, mb, mh, mhb, a_out, gx_out, u_out, gh_out, f_hi, f_lo, latent, chosen, chosen_hl, cbg,
    x_ref, z0, z1, clip_ref, e_ref, o_ref, d_ref, ids_ref,
):
    sel = selector()
    x_ref[:, :CORE] = frames[...]
    x_ref[:, CORE : CORE + HALO] = hi[:CH]
    x_ref[:, CORE + HALO :] = lo[:CH]
    clip_ref[:, :CORE] = jnp.broadcast_to(clip[...].astype(F32), (8, CORE))
    clip_ref[:, CORE : CORE + HALO] = jnp.broadcast_to(hi[128:129], (8, HALO))
    clip_ref[:, CORE + HALO :] = jnp.broadcast_to(lo[128:129], (8, HALO))
    ids_ref[:, :HCORE] = jnp.broadcast_to(codes[...], (8, HCORE))
    ids_ref[:, HCORE:] = jnp.broadcast_to((hi[129:130] + lo[129:130]).astype(jnp.int32), (8, HALO))

    def links(start, size, core):
        at = pl.ds(aligned(start), size)
        here = lanes(clip_ref, start, size)

        def same(other):
            return jnp.where(other == here, 1.0, 0.0)

        for m, d in enumerate(DILATIONS):
            left = same(from_left(clip_ref, slice(None), start, size, d, EXT))
            right = same(from_right(clip_ref, slice(None), start, size, d, EXT))
            mf[16 * m : 16 * m + 8, at] = left
            mf[16 * m + 8 : 16 * m + 16, at] = right
            mb[32 * m : 32 * m + 16, at] = tile_rows(left, 2).astype(BF)
            mb[32 * m + 16 : 32 * m + 32, at] = tile_rows(right, 2).astype(BF)
            if m == 0:
                two = same(from_right(clip_ref, slice(None), start, size, 2, EXT))
                rows = jnp.concatenate([left, right, two, two], axis=0).astype(BF)
                half = start // 2
                for i in range(size // 256):
                    out = dot(rows[:, i * 256 : (i + 1) * 256], sel)[:, :128]
                    hat = pl.ds(aligned(half + 128 * i), 128)
                    mh[:, hat] = out[:24]
                    for n in range(3):
                        mhb[16 * n : 16 * n + 16, hat] = tile_rows(
                            out[8 * n : 8 * n + 8], 2
                        ).astype(BF)

    sweep(links)

    def pick(start, size, core):
        at = pl.ds(aligned(start), size)
        both = dot(cbt[...], one_hot(lanes(ids_ref, start, size, slice(0, 1)), 0, CODES))
        chosen[:, at] = both[:CH] + both[CH:]
        chosen_hl[:, at] = both.astype(BF)

    half_sweep(pick)

    def keep(b):
        return a_out.at[b], gx_out.at[b], u_out.at[b], gh_out.at[b]

    def last(out, start, size, core):
        to_halves(out, sel, e_ref, o_ref, start, size)

    stack_forward(x_ref, (z0, z1), 0, DILATIONS, wf, pf, bias, mf, keep, last)

    def down(start, size, core):
        at = pl.ds(aligned(start), size)
        parts = pair_stack(e_ref, o_ref, mhb, start, size)
        value = pair_gather(dg, parts) + jnp.concatenate([bias[16]] * (size // 128), axis=1)
        latent[:, at] = value
        if core:
            f_hi[:, at] = parts[0]
            f_lo[:, at] = parts[1]
            dhi, dlo = split(2.0 * (lanes(chosen, start, size) - value))
            d_ref[:CH, at] = dhi
            d_ref[CH:, at] = dlo

    half_sweep(down)

    def codes_back(i, carry):
        parts = []
        for side in range(2):
            hot = one_hot(ids_ref[0:1, :HCORE], i * 256 + side * (CODES // 2), 256)
            out = dot_nt(hot, d_ref[...])
            parts.append(out[:, :CH] + out[:, CH:])
        cbg[pl.ds(pl.multiple_of(i * 256, 256), 256), :] = jnp.concatenate(parts, axis=1)
        return carry

    lax.fori_loop(0, CODES // 512, codes_back, 0)


def sum_refs():
    return [
        pltpu.VMEM((4, 3 * CH, 2 * CH), F32),
        pltpu.VMEM((4, 3 * CH, CH), F32),
        pltpu.VMEM((4, 2 * CH, 2 * CH), F32),
        pltpu.VMEM((4, CH, 128), F32),
        pltpu.VMEM((4, CH, 128), F32),
    ]


def decode_kernel(
    cot, lo, hi, chosen_hl, mf, mb, mh, mhb, wf, wb, pf, pb, ug, us, bias,
    rebuilt, quant_grad, grads,
    x_ref, z0, z1, zu, a_s, gx_s, u_s, gh_s, g0, g1, e_ref, o_ref, up1, up2, usum, *acc,
):
    sel = selector()
    spread(us, chosen_hl, mh, zu, sel, bias[17], x_ref)

    def keep(b):
        return a_s.at[b], gx_s.at[b], u_s.at[b], gh_s.at[b]

    def last(out, start, size, core):
        if core:
            rebuilt[:, pl.ds(aligned(start), size)] = out

    order = DILATIONS[::-1]
    stack_forward(x_ref, (z0, z1), 4, order, wf, pf, bias, mf, keep, last)
    x_ref[:, :CORE] = cot[...]
    x_ref[:, CORE : CORE + HALO] = hi[CH : 2 * CH]
    x_ref[:, CORE + HALO :] = lo[CH : 2 * CH]
    for ref in (up1, up2, usum):
        ref[...] = jnp.zeros(ref.shape, F32)
    grads[GRAD_BIAS:, :] = jnp.zeros((CH, 128), F32)

    def last_back(out, start, size, core):
        to_halves(out, sel, e_ref, o_ref, start, size)
        if core:
            usum[...] += lane_fold(out)

    stack_backward(
        x_ref, (g0, g1), 4, order, wb, pb, mb, keep, acc, store_grads(grads), last_back
    )

    def up(start, size, core):
        parts = pair_stack(e_ref, o_ref, mhb, start, size)
        quant_grad[:, pl.ds(aligned(start), size)] = pair_gather(ug, parts)
        if core:
            both = lanes(chosen_hl, start, size)
            up1[...] += dot_nt(parts[0], both)
            up2[...] += dot_nt(parts[1], both[:CH])

    half_sweep(up)
    total = up1[:, :CH] + up1[:, CH:] + up2[...]
    grads[GRAD_PAIR:GRAD_BIAS, :] = jnp.concatenate([total[: 2 * CH], total[2 * CH :]], axis=1)
    put_column(grads, 8, usum[...])


def encode_back_kernel(
    latent, chosen, quant_grad, f_hi, f_lo, a_in, gx_in, u_in, gh_in, mb, mh, wb, pb, ds_,
    frames_grad, grads,
    x_ref, zu, l_ref, g0, g1, down1, down2, dsum, *acc,
):
    sel = selector()
    for ref in (down1, down2, dsum):
        ref[...] = jnp.zeros(ref.shape, F32)
    grads[GRAD_BIAS:, :] = jnp.zeros((CH, 128), F32)

    def first(start, size, core):
        at = pl.ds(aligned(start), size)
        value = quant_grad[:, at] + (2.0 * COMMIT) * (latent[:, at] - chosen[:, at])
        hi, lo = split(value)
        l_ref[:CH, at] = hi
        l_ref[CH:, at] = lo
        if core:
            dsum[...] += lane_fold(value)
            fh = f_hi[:, at]
            down1[...] += dot_nt(jnp.concatenate([hi, lo], axis=0), fh)
            down2[...] += dot_nt(hi, f_lo[:, at])

    half_sweep(first)
    spread(ds_, l_ref, mh, zu, sel, None, x_ref)

    def keep(b):
        return a_in.at[b], gx_in.at[b], u_in.at[b], gh_in.at[b]

    def last(out, start, size, core):
        if core:
            frames_grad[:, pl.ds(aligned(start), size)] = out

    stack_backward(
        x_ref, (g0, g1), 0, DILATIONS, wb, pb, mb, keep, acc, store_grads(grads), last
    )
    total = down1[:CH] + down1[CH:] + down2[...]
    grads[GRAD_PAIR : GRAD_PAIR + CH, :] = total[:, : 2 * CH]
    grads[GRAD_PAIR + CH : GRAD_BIAS, :] = total[:, 2 * CH :]
    put_column(grads, 8, dsum[...])


def unpack_kernel(
    enc, dec, cb,
    ec, ecb, ep, epb, dw, db, cg, uw, ub, dc, dcb, dp, dpb,
):
    for src, conv, cbias, proj, pbias, single in (
        (enc, ec, ecb, ep, epb, db),
        (dec, dc, dcb, dp, dpb, ub),
    ):
        rows = src[GRAD_BIAS:, :].T
        for b in range(4):
            at = slice((b % 2) * CH, (b % 2 + 1) * CH)
            p = b // 2
            conv[b] = src[p * 192 : (p + 1) * 192, at].reshape(3, CH, CH)
            proj[b] = src[GRAD_PROJ + p * CH : GRAD_PROJ + (p + 1) * CH, at]
            cbias[b : b + 1, :] = rows[2 * b : 2 * b + 1]
            pbias[b : b + 1, :] = rows[2 * b + 1 : 2 * b + 2]
        single[...] = rows[8:9]
    for k in range(4):
        a, b = k // 2, k % 2
        dw[k] = enc[GRAD_PAIR + a * CH : GRAD_PAIR + (a + 1) * CH, b * CH : (b + 1) * CH]
        uw[k] = dec[GRAD_PAIR + b * CH : GRAD_PAIR + (b + 1) * CH, a * CH : (a + 1) * CH]
    cg[: CODES // 2, :] = cb[:, :CH]
    cg[CODES // 2 :, :] = cb[:, CH:]


def shape(dims, kind=F32):
    return jax.ShapeDtypeStruct(dims, kind)


def call(kernel, outs, scratch=(), flops=0, limit=56):
    return pl.pallas_call(
        kernel,
        out_shape=outs,
        scratch_shapes=list(scratch),
        compiler_params=pltpu.CompilerParams(vmem_limit_bytes=limit * MB),
        cost_estimate=pl.CostEstimate(flops=flops, bytes_accessed=2**22, transcendentals=0),
    )


def halves(kind=BF, rows=2 * CH):
    return pltpu.VMEM((rows, HEXT), kind)


def whole(kind=F32, rows=CH):
    return pltpu.VMEM((rows, EXT), kind)


def local_prep(ec, ecb, ep, epb, dw, db, cb, uw, ub, dc, dcb, dp, dpb):
    return call(
        prep_kernel,
        [
            shape((8, 192, 192), BF),
            shape((8, 128, 192), BF),
            shape((8, 64, 192), BF),
            shape((8, 64, 192), BF),
            shape((128, 256), BF),
            shape((256, 192), BF),
            shape((128, 256), BF),
            shape((256, 192), BF),
            shape((128, CODES), BF),
            shape((18, CH, 128)),
        ],
    )(ec, ecb, ep, epb, dw, db.reshape(1, CH), cb, uw, ub.reshape(1, CH), dc, dcb, dp, dpb)


def local_encode(frames, lo, hi, clip, codes, wf, pf, dg, cbt, bias):
    return call(
        encode_kernel,
        [
            shape((64, EXT)),
            shape((128, EXT), BF),
            shape((24, HEXT)),
            shape((48, HEXT), BF),
            shape((4, 128, EXT), BF),
            shape((4, 64, EXT)),
            shape((4, 128, EXT), BF),
            shape((4, 64, EXT)),
            shape((256, HCORE), BF),
            shape((256, HCORE), BF),
            shape((CH, HEXT)),
            shape((CH, HEXT)),
            shape((2 * CH, HEXT), BF),
            shape((CODES // 2, 128)),
        ],
        [
            whole(),
            whole(rows=192),
            whole(rows=192),
            whole(rows=8),
            halves(),
            halves(),
            pltpu.VMEM((2 * CH, HCORE), BF),
            pltpu.VMEM((8, HEXT), jnp.int32),
        ],
        flops=10**10,
    )(frames, lo, hi, clip, codes, wf, pf, dg, cbt, bias)


def local_decode(cot, lo, hi, chosen_hl, mf, mb, mh, mhb, wf, wb, pf, pb, ug, us, bias):
    return call(
        decode_kernel,
        [shape((CH, CORE)), shape((CH, HEXT)), shape((GRAD_ROWS, 128))],
        [
            whole(),
            whole(rows=192),
            whole(rows=192),
            halves(F32, 256),
            pltpu.VMEM((4, 128, EXT), BF),
            pltpu.VMEM((4, CH, EXT), F32),
            pltpu.VMEM((4, 128, EXT), BF),
            pltpu.VMEM((4, CH, EXT), F32),
            whole(BF, 128),
            whole(BF, 128),
            halves(),
            halves(),
            pltpu.VMEM((256, 128), F32),
            pltpu.VMEM((256, CH), F32),
            pltpu.VMEM((CH, 128), F32),
            *sum_refs(),
        ],
        flops=2 * 10**10,
    )(cot, lo, hi, chosen_hl, mf, mb, mh, mhb, wf, wb, pf, pb, ug, us, bias)


def local_encode_back(latent, chosen, quant_grad, f_hi, f_lo, a, gx, u, gh, mb, mh, wb, pb, ds_):
    return call(
        encode_back_kernel,
        [shape((CH, CORE)), shape((GRAD_ROWS, 128))],
        [
            whole(),
            halves(F32, 256),
            halves(),
            whole(BF, 128),
            whole(BF, 128),
            pltpu.VMEM((128, 256), F32),
            pltpu.VMEM((CH, 256), F32),
            pltpu.VMEM((CH, 128), F32),
            *sum_refs(),
        ],
        flops=10**10,
    )(latent, chosen, quant_grad, f_hi, f_lo, a, gx, u, gh, mb, mh, wb, pb, ds_)


def local_unpack(enc, dec, cb):
    block = [shape((4, 3, CH, CH)), shape((4, CH)), shape((4, CH, CH)), shape((4, CH))]
    return call(
        unpack_kernel,
        [
            *block,
            shape((4, CH, CH)),
            shape((1, CH)),
            shape((CODES, CH)),
            shape((4, CH, CH)),
            shape((1, CH)),
            *block,
        ],
    )(enc, dec, cb)


def edges(frames, cotangent, clip, codes):
    count = lax.axis_size("tm")
    me = lax.axis_index("tm")

    def packed(cut, half, after, at_end):
        clip_row = jnp.where(at_end, -1.0, clip[:, cut].astype(F32))
        code_row = jnp.pad(codes[:, half].astype(F32), ((0, 0), after))
        blank = jnp.zeros((6, HALO), F32)
        return jnp.concatenate(
            [frames[:, cut], cotangent[:, cut], clip_row, code_row, blank], axis=0
        )

    tail = packed(slice(CORE - HALO, CORE), slice(HCORE - 64, HCORE), (64, 0), me == count - 1)
    front = packed(slice(0, HALO), slice(0, 64), (0, 64), me == 0)
    ring = [(i, (i + 1) % count) for i in range(count)]
    back = [(j, i) for i, j in ring]
    return lax.ppermute(tail, "tm", ring), lax.ppermute(front, "tm", back)


def turn(axis, stride, size, shift):
    count = lax.axis_size(axis)
    pairs = []
    for i in range(count):
        digit = i // stride % size
        pairs.append((i, i + ((digit + shift) % size - digit) * stride))
    return pairs


def digits():
    tm = lax.axis_size("tm")
    out = [("tm", 1, 2)]
    stride = 2
    while stride < tm:
        size = min(4, tm // stride)
        out.append(("tm", stride, size))
        stride *= size
    return out


def exchange(value, axis, stride, size):
    if size == 2:
        return value + lax.ppermute(value, axis, turn(axis, stride, 2, 1))
    got = [lax.ppermute(value, axis, turn(axis, stride, 4, s)) for s in (1, 2, 3)]
    return (value + got[1]) + (got[0] + got[2])


def sum_all(value):
    rows = value.shape[0]
    for digit in digits()[:1]:
        value = exchange(value, *digit)
    size = lax.axis_size("batch")
    part = rows // size
    me = lax.axis_index("batch")

    def cut(s):
        return lax.dynamic_slice_in_dim(value, lax.rem(me + s, size) * part, part, 0)

    got = [
        lax.ppermute(cut(s), "batch", [(i, (i + s) % size) for i in range(size)])
        for s in range(1, size)
    ]
    if size == 4:
        mine = (cut(0) + got[1]) + (got[0] + got[2])
    else:
        mine = cut(0) + got[0]
    for digit in digits()[1:]:
        mine = exchange(mine, *digit)
    out = jnp.zeros_like(value)
    out = lax.dynamic_update_slice_in_dim(out, mine, me * part, 0)
    for s in range(1, size):
        other = lax.ppermute(mine, "batch", [(i, (i + s) % size) for i in range(size)])
        out = lax.dynamic_update_slice_in_dim(out, other, lax.rem(me + size - s, size) * part, 0)
    return out


def on_device(
    frames, clip_start, code_ids, cotangent,
    enc_conv, enc_conv_bias, enc_proj, enc_proj_bias, downscale_weight, downscale_bias,
    codebook, up_weight, up_bias, dec_conv, dec_conv_bias, dec_proj, dec_proj_bias,
):
    frames = frames.reshape(CH, CORE)
    cotangent = cotangent.reshape(CH, CORE)
    lo, hi = edges(frames, cotangent, clip_start, code_ids)
    wf, wb, pf, pb, dg, ds_, ug, us, cbt, bias = local_prep(
        enc_conv, enc_conv_bias, enc_proj, enc_proj_bias, downscale_weight, downscale_bias,
        codebook, up_weight, up_bias, dec_conv, dec_conv_bias, dec_proj, dec_proj_bias,
    )
    (mf, mb, mh, mhb, a, gx, u, gh, f_hi, f_lo, latent, chosen, chosen_hl, cbg) = local_encode(
        frames, lo, hi, clip_start, code_ids, wf, pf, dg, cbt, bias
    )
    cb_sum = sum_all(cbg)
    rebuilt, quant_grad, dec_grads = local_decode(
        cotangent, lo, hi, chosen_hl, mf, mb, mh, mhb, wf, wb, pf, pb, ug, us, bias
    )
    dec_sum = sum_all(dec_grads)
    frames_grad, enc_grads = local_encode_back(
        latent, chosen, quant_grad, f_hi, f_lo, a, gx, u, gh, mb, mh, wb, pb, ds_
    )
    enc_sum = sum_all(enc_grads)
    out = list(local_unpack(enc_sum, dec_sum, cb_sum))
    out[5] = out[5].reshape(CH)
    out[8] = out[8].reshape(CH)
    return (rebuilt[None], frames_grad[None], *out)


def solution(mesh):
    split_spec = P("batch", None, "tm")
    row_spec = P("batch", "tm")
    return jax.shard_map(
        on_device,
        mesh=mesh,
        in_specs=(split_spec, row_spec, row_spec, split_spec) + (P(),) * 13,
        out_specs=(split_spec, split_spec) + (P(),) * 13,
        check_vma=False,
    )
```

time: 706 us -> 230 us (0.33); the launches traced: 697 us -> 229 us
  local copies, waits for them, and re-layouts: 198 us -> 7.36 us
  matrix products: 184 us -> 0 us
  Pallas kernels: 0 us -> 139 us
  blocking collectives: 78.1 us -> 0 us
  waiting for transfers between devices: 98.2 us -> 27.4 us
  starting transfers between devices: 91.5 us -> 51.3 us
  other arithmetic: 30.3 us -> 2.82 us
  between operations: 17.2 us -> 1.01 us
    dot_general x120 -> x0, matrix products: 184 us -> none  [the longest x48 71.4 us: matmul(): jnp.einsum('oi,wit->wot', weight, value_entries, precision=lax.Precision....]
    slice x28 -> x1, local copies, waits for them, and re-layouts: 153 us -> 0.82 us  [packed(): cotangent[:, cut]]
    pallas_call x0 -> x5, Pallas kernels: none -> 139 us  [the longest x1 53.6 us: local_decode(): call(decode_kernel, [shape((CH, CORE)), shape((CH, HEXT)), shape((GRAD_RO...]
    psum x1 -> x0, waiting for transfers between devices: 81.8 us -> none  [on_device(): lax.psum((enc_grads[0], enc_grads[1], enc_grads[2], enc_grads[3], down_gr...]
    psum x1 -> x0, blocking collectives: 78.1 us -> none  [on_device(): lax.psum((enc_grads[0], enc_grads[1], enc_grads[2], enc_grads[3], down_gr...]
    ppermute x30 -> x41, starting transfers between devices: 91.5 us -> 51.3 us  [the longest x18 22.3 us: exchange(): lax.ppermute(value, axis, turn(axis, stride, 4, s))]
    scatter-add x1 -> x0, other arithmetic: 13 us -> none  [on_device(): jax.ops.segment_sum(code_terms, code_ids.reshape(-1), num_segments=codebo...]
    concatenate x6 -> x2, local copies, waits for them, and re-layouts: 11.2 us -> 0.05 us  [packed(): jnp.concatenate([frames[:, cut], cotangent[:, cut], clip_row, code_row, b...]
  transfers between devices with their start and end apart: 31 -> 41, of which waited for: 7 -> 16; matrix products, arithmetic and copies ran while one was open for 25% -> 2% of each run, Pallas kernels for 0% -> 2%
where the time goes in v1:
time: 230 us; the launch traced here: 229 us
  Pallas kernels  139 us (60%)
  starting transfers between devices  51.3 us (22%)
  waiting for transfers between devices  27.4 us (12%)
  local copies, waits for them, and re-layouts  7.36 us (3%)
  other arithmetic  2.82 us (1%)
    pallas_call x1, Pallas kernels, local_decode(): call(decode_kernel, [shape((CH, CORE)), shape((CH, HEXT)), shape((GRAD_RO...  53.6 us
    pallas_call x1, Pallas kernels, local_encode(): call(encode_kernel, [shape((64, EXT)), shape((128, EXT), BF), shape((24,...  43.1 us
    pallas_call x1, Pallas kernels, local_encode_back(): call(encode_back_kernel, [shape((CH, CORE)), shape((GRAD_ROWS, 128))], [w...  35.6 us
    ppermute x18, starting transfers between devices, exchange(): lax.ppermute(value, axis, turn(axis, stride, 4, s))  22.3 us
    ppermute x18, waiting for transfers between devices, exchange(): lax.ppermute(value, axis, turn(axis, stride, 4, s))  18.7 us
    ppermute x9, starting transfers between devices, sum_all(): lax.ppermute(cut(s), 'batch', [(i, (i + s) % size) for i in range(size)])  13.7 us
    ppermute x9, starting transfers between devices, sum_all(): lax.ppermute(mine, 'batch', [(i, (i + s) % size) for i in range(size)])  8.58 us
    ppermute x2, starting transfers between devices, edges(): return (lax.ppermute(tail, 'tm', ring), lax.ppermute(front, 'tm', back))  6.14 us
  transfers between devices with their start and end apart: 41, of which 16 were waited for; matrix products, arithmetic and copies ran while one was open for 2% of the time, Pallas kernels for 2%

profile of v1, /device:TPU:0, one launch (start us, length us, event | category | flops | bytes accessed | tf_op | source)
XLA Modules:
  0.0 229.3 jit_solution(11978635900234694558)
XLA Ops:
  0.7 0.7 slice_convert_fusion
  1.4 0.8 fusion
  3.1 6.1 %collective-permute-start.1 = (f32[136,128]{1,0:T(8,128)S(1)}, f32[136,128]{1,0:T(8,128)S(1)}, u32[]{:S(2)}, u32[]{:S(2)}) collective-permute-start(f32[136,128]{1,0:T(8,128)S(1)} %concatenate.7), channel_id=1, source_target_pairs={{4,0},{8,4},{12,8},{16,12},{20,16},{24,20},{28,24},{32,28},{36,32}... | collective-permute-start | bytes 208904 | tf_op jit(solution)/shard_map/ppermute | solution.py:722
  9.2 2.4 %copy.32.cb = f32[2048,64]{1,0:T(8,128)} copy(f32[2048,64]{0,1:T(8,128)} %param.27) | data formatting | bytes 1048576 | tf_op args[10]
  11.5 4.2 %shard_map.280 = (bf16[8,192,192]{2,1,0:T(8,128)(2,1)}, bf16[8,128,192]{2,1,0:T(8,128)(2,1)}, bf16[8,64,192]{2,1,0:T(8,128)(2,1)}, bf16[8,64,192]{2,1,0:T(8,128)...) custom-call(f32[4,3,64,64]{3,2,1,0:T(8,128)} %ec.1, ...), custom_call_target="tpu_custom_call" | custom-call | bytes 4194304 | tf_op jit(solution)/shard_map/pallas_call | solution.py:595
  16.4 43.1 %shard_map.281 = (f32[64,4352]{1,0:T(8,128)}, bf16[128,4352]{1,0:T(8,128)(2,1)}, f32[24,2176]{1,0:T(8,128)}, bf16[48,2176]{1,0:T(8,128)(2,1)}, bf16[4,128,4352]{...) custom-call(f32[64,4096]{1,0:T(8,128)} %bitcast.9, ...), custom_call_target="tpu_custom_call" | custom-call | flops 10000000000 | bytes 4194304 | tf_op jit(solution)/shard_map/pallas_call | solution.py:613
  59.5 53.6 %shard_map.282 = (f32[64,4096]{1,0:T(8,128)}, f32[64,2176]{1,0:T(8,128)}, f32[704,128]{1,0:T(8,128)}) custom-call(f32[64,4096]{1,0:T(8,128)} %bitcast.11, f32[136,128]{1,0:T(8,128)} %copy-done.5, f32[136,128]{1,0:T(8,128)} %copy-done.6, bf16[128,2176]{1,0:T(8,128)(2,1)} %get-tuple-element.62.chosen_hl, f32[64,4352]{1,0:T(8,128)} %get-tuple-element.63.mf, ...), custom_call_target="tpu_custom_call" | custom-call | flops 20000000000 | bytes 4194304 | tf_op jit(solution)/shard_map/pallas_call | solution.py:646
  113.0 35.6 %shard_map.283 = (f32[64,4096]{1,0:T(8,128)}, f32[704,128]{1,0:T(8,128)}) custom-call(f32[64,2176]{1,0:T(8,128)} %get-tuple-element.72.latent, f32[64,2176]{1,0:T(8,128)} %get-tuple-element.73.chosen, f32[64,2176]{1,0:T(8,128)} %get-tuple-element.74.quant_grad, bf16[256,2048]{1,0:T(8,128)(2,1)} %get-tuple-element.75.f_hi, ...), custom_call_target="tpu_custom_call" | custom-call | flops 10000000000 | bytes 4194304 | tf_op jit(solution)/shard_map/pallas_call | solution.py:672
  149.2 1.3 collective-permute-done.2
  150.5 1.0 add.171
  151.6 1.5 collective-permute-start.4
  153.1 1.8 collective-permute-start.5
  154.9 1.8 collective-permute-start.3
  157.5 2.6 %collective-permute-start.18 = (f32[176,128]{1,0:T(8,128)S(1)}, f32[176,128]{1,0:T(8,128)S(1)}, u32[]{:S(2)}, u32[]{:S(2)}) collective-permute-start(f32[176,128]{1,0:T(8,128)S(1)} %get-tuple-element.128), channel_id=1, source_target_pairs={{0,3},{1,0},{2,1},{3,2},{4,7},{5,4},{6,5},{7,6},{8,11},{9,8},{10,9... | collective-permute-start | bytes 270344 | tf_op jit(solution)/shard_map/ppermute | solution.py:764
  160.1 1.3 collective-permute-start.16
  161.7 1.2 collective-permute-done.17
  162.8 2.1 collective-permute-start.8
  164.9 1.2 collective-permute-done.16
  166.2 3.2 %collective-permute-start.21 = (f32[176,128]{1,0:T(8,128)S(1)}, f32[176,128]{1,0:T(8,128)S(1)}, u32[]{:S(2)}, u32[]{:S(2)}) collective-permute-start(f32[176,128]{1,0:T(8,128)S(1)} %add_add_fusion.5), channel_id=1, source_target_pairs={{0,24},{4,28},{8,0},{12,4},{16,8},{20,12},{24,16},{28,20},{32,56},... | collective-permute-start | bytes 270344 | tf_op jit(solution)/shard_map/ppermute | solution.py:748
  169.6 1.2 collective-permute-start.19
  170.8 1.5 collective-permute-start.30
  172.3 1.8 collective-permute-start.31
  174.1 3.2 %collective-permute-start.11 = (f32[176,128]{1,0:T(8,128)S(1)}, f32[176,128]{1,0:T(8,128)S(1)}, u32[]{:S(2)}, u32[]{:S(2)}) collective-permute-start(f32[176,128]{1,0:T(8,128)S(1)} %add_add_fusion.7), channel_id=1, source_target_pairs={{0,96},{4,100},{8,104},{12,108},{16,112},{20,116},{24,120},{28,124... | collective-permute-start | bytes 270344 | tf_op jit(solution)/shard_map/ppermute | solution.py:748
  177.4 3.3 %collective-permute-done.10 = f32[176,128]{1,0:T(8,128)S(1)} collective-permute-done((f32[176,128]{1,0:T(8,128)S(1)}, f32[176,128]{1,0:T(8,128)S(1)}, u32[]{:S(2)}, u32[]{:S(2)}) %collective-permute-start.10) | collective-permute-done | bytes 90144 | tf_op jit(solution)/shard_map/ppermute | solution.py:748
  180.7 1.0 collective-permute-done.11
  181.7 3.8 %collective-permute-start.24 = (f32[176,128]{1,0:T(8,128)S(1)}, f32[176,128]{1,0:T(8,128)S(1)}, u32[]{:S(2)}, u32[]{:S(2)}) collective-permute-start(f32[176,128]{1,0:T(8,128)S(1)} %add_add_fusion.4), channel_id=1, source_target_pairs={{0,96},{4,100},{8,104},{12,108},{16,112},{20,116},{24,120},{28,124... | collective-permute-start | bytes 270344 | tf_op jit(solution)/shard_map/ppermute | solution.py:748
  185.7 0.8 collective-permute-done.23
  186.4 0.8 collective-permute-start.29
  187.3 1.4 collective-permute-done.24
  188.7 2.9 %collective-permute-done.22 = f32[176,128]{1,0:T(8,128)S(1)} collective-permute-done((f32[176,128]{1,0:T(8,128)S(1)}, f32[176,128]{1,0:T(8,128)S(1)}, u32[]{:S(2)}, u32[]{:S(2)}) %collective-permute-start.22) | collective-permute-done | bytes 90144 | tf_op jit(solution)/shard_map/ppermute | solution.py:748
  191.6 0.9 collective-permute-start.13
  192.6 1.9 collective-permute-start.14
  194.6 3.2 %collective-permute-start.34 = (f32[256,128]{1,0:T(8,128)S(1)}, f32[256,128]{1,0:T(8,128)S(1)}, u32[]{:S(2)}, u32[]{:S(2)}) collective-permute-start(f32[256,128]{1,0:T(8,128)S(1)} %add_add_fusion.2), channel_id=1, source_target_pairs={{0,24},{4,28},{8,0},{12,4},{16,8},{20,12},{24,16},{28,20},{32,56},... | collective-permute-start | bytes 393224 | tf_op jit(solution)/shard_map/ppermute | solution.py:748
  197.8 0.8 collective-permute-start.32
  198.8 2.0 collective-permute-done.33
  200.8 1.3 collective-permute-start.26
  202.1 2.2 collective-permute-done.32
  204.7 3.2 %collective-permute-start.37 = (f32[256,128]{1,0:T(8,128)S(1)}, f32[256,128]{1,0:T(8,128)S(1)}, u32[]{:S(2)}, u32[]{:S(2)}) collective-permute-start(f32[256,128]{1,0:T(8,128)S(1)} %add_add_fusion.1), channel_id=1, source_target_pairs={{0,96},{4,100},{8,104},{12,108},{16,112},{20,116},{24,120},{28,124... | collective-permute-start | bytes 393224 | tf_op jit(solution)/shard_map/ppermute | solution.py:748
  207.9 0.9 collective-permute-start.35
  209.4 1.4 collective-permute-done.36
  210.9 3.5 %collective-permute-done.35 = f32[256,128]{1,0:T(8,128)S(1)} collective-permute-done((f32[256,128]{1,0:T(8,128)S(1)}, f32[256,128]{1,0:T(8,128)S(1)}, u32[]{:S(2)}, u32[]{:S(2)}) %collective-permute-start.35) | collective-permute-done | bytes 131104 | tf_op jit(solution)/shard_map/ppermute | solution.py:748
  214.8 2.7 %collective-permute-start.39 = (f32[256,128]{1,0:T(8,128)S(1)}, f32[256,128]{1,0:T(8,128)S(1)}, u32[]{:S(2)}, u32[]{:S(2)}) collective-permute-start(f32[256,128]{1,0:T(8,128)S(1)} %get-tuple-element.115), channel_id=1, source_target_pairs={{0,2},{1,3},{2,0},{3,1},{4,6},{5,7},{6,4},{7,5},{8,10},{9,11},{10,... | collective-permute-start | bytes 393224 | tf_op jit(solution)/shard_map/ppermute | solution.py:776
  217.5 0.8 collective-permute-start.40
  218.3 3.8 %collective-permute-done.38 = f32[256,128]{1,0:T(8,128)S(1)} collective-permute-done((f32[256,128]{1,0:T(8,128)S(1)}, f32[256,128]{1,0:T(8,128)S(1)}, u32[]{:S(2)}, u32[]{:S(2)}) %collective-permute-start.38) | collective-permute-done | bytes 131104 | tf_op jit(solution)/shard_map/ppermute | solution.py:776
  222.2 0.9 collective-permute-done.40
  223.1 0.8 copy-done
  223.9 3.0 %shard_map.284 = (f32[4,3,64,64]{3,2,1,0:T(8,128)}, f32[4,64]{1,0:T(4,128)}, f32[4,64,64]{2,1,0:T(8,128)}, f32[4,64]{1,0:T(4,128)}, f32[4,64,64]{2,1,0:T(8,128)}...) custom-call(f32[704,128]{1,0:T(8,128)} %copy-done.2, ...), custom_call_target="tpu_custom_call" | custom-call | bytes 4194304 | tf_op jit(solution)/shard_map/pallas_call | solution.py:692
  227.0 2.3 %copy.33 = f32[2048,64]{0,1:T(8,128)} copy(f32[2048,64]{1,0:T(8,128)} %get-tuple-element.107) | data formatting | bytes 1048576
  (90 shorter events, 5.4 us)
Async XLA Ops:
  3.0 12.7 %collective-permute-start = (f32[136,128]{1,0:T(8,128)S(1)}, f32[136,128]{1,0:T(8,128)S(1)}, u32[]{:S(2)}, u32[]{:S(2)}) collective-permute-start(f32[136,128]{1,0:T(8,128)S(1)} %concatenate.6), channel_id=1, source_target_pairs={{0,4},{4,8},{8,12},{12,16},{16,20},{20,24},{24,28},{28,32},{32,36}... | collective-permute-start | bytes 208904 | tf_op jit(solution)/shard_map/ppermute | solution.py:722
  3.1 12.6 %collective-permute-start.1 = (f32[136,128]{1,0:T(8,128)S(1)}, f32[136,128]{1,0:T(8,128)S(1)}, u32[]{:S(2)}, u32[]{:S(2)}) collective-permute-start(f32[136,128]{1,0:T(8,128)S(1)} %concatenate.7), channel_id=1, source_target_pairs={{4,0},{8,4},{12,8},{16,12},{20,16},{24,20},{28,24},{32,28},{36,32}... | collective-permute-start | bytes 208904 | tf_op jit(solution)/shard_map/ppermute | solution.py:722
  15.7 0.6 copy-start.5
  15.8 0.6 copy-start.6
  113.0 35.6 %copy-start.4 = (f32[704,128]{1,0:T(8,128)S(1)}, f32[704,128]{1,0:T(8,128)}, u32[]{:S(2)}) copy-start(f32[704,128]{1,0:T(8,128)} %get-tuple-element.84) | copy-start | bytes 1081348
  113.0 36.1 %copy-start.3 = (f32[1024,128]{1,0:T(8,128)S(1)}, f32[1024,128]{1,0:T(8,128)}, u32[]{:S(2)}) copy-start(f32[1024,128]{1,0:T(8,128)} %get-tuple-element.85) | copy-start | bytes 1572868
  148.6 1.9 collective-permute-start.2
  148.6 8.1 %collective-permute-start.15 = (f32[704,128]{1,0:T(8,128)S(1)}, f32[704,128]{1,0:T(8,128)S(1)}, u32[]{:S(2)}, u32[]{:S(2)}) collective-permute-start(f32[704,128]{1,0:T(8,128)S(1)} %copy-done.4), channel_id=1, source_target_pairs={{0,4},{4,0},{8,12},{12,8},{16,20},{20,16},{24,28},{28,24},{32,36},... | collective-permute-start | bytes 1081352 | tf_op jit(solution)/shard_map/ppermute | solution.py:747
  149.1 17.1 %collective-permute-start.28 = (f32[1024,128]{1,0:T(8,128)S(1)}, f32[1024,128]{1,0:T(8,128)S(1)}, u32[]{:S(2)}, u32[]{:S(2)}) collective-permute-start(f32[1024,128]{1,0:T(8,128)S(1)} %copy-done.3), channel_id=1, source_target_pairs={{0,4},{4,0},{8,12},{12,8},{16,20},{20,16},{24,28},{28,24},{32,36},... | collective-permute-start | bytes 1572872 | tf_op jit(solution)/shard_map/ppermute | solution.py:747
  151.6 5.9 %collective-permute-start.4 = (f32[176,128]{1,0:T(8,128)S(1)}, f32[176,128]{1,0:T(8,128)S(1)}, u32[]{:S(2)}, u32[]{:S(2)}) collective-permute-start(f32[176,128]{1,0:T(8,128)S(1)} %get-tuple-element.132), channel_id=1, source_target_pairs={{0,1},{1,2},{2,3},{3,0},{4,5},{5,6},{6,7},{7,4},{8,9},{9,10},{10,1... | collective-permute-start | bytes 270344 | tf_op jit(solution)/shard_map/ppermute | solution.py:764
  153.1 7.0 %collective-permute-start.5 = (f32[176,128]{1,0:T(8,128)S(1)}, f32[176,128]{1,0:T(8,128)S(1)}, u32[]{:S(2)}, u32[]{:S(2)}) collective-permute-start(f32[176,128]{1,0:T(8,128)S(1)} %get-tuple-element.131), channel_id=1, source_target_pairs={{0,3},{1,0},{2,1},{3,2},{4,7},{5,4},{6,5},{7,6},{8,11},{9,8},{10,9... | collective-permute-start | bytes 270344 | tf_op jit(solution)/shard_map/ppermute | solution.py:764
  154.9 6.7 %collective-permute-start.3 = (f32[176,128]{1,0:T(8,128)S(1)}, f32[176,128]{1,0:T(8,128)S(1)}, u32[]{:S(2)}, u32[]{:S(2)}) collective-permute-start(f32[176,128]{1,0:T(8,128)S(1)} %get-tuple-element.130), channel_id=1, source_target_pairs={{0,2},{1,3},{2,0},{3,1},{4,6},{5,7},{6,4},{7,5},{8,10},{9,11},{10,... | collective-permute-start | bytes 270344 | tf_op jit(solution)/shard_map/ppermute | solution.py:764
  156.8 6.1 %collective-permute-start.17 = (f32[176,128]{1,0:T(8,128)S(1)}, f32[176,128]{1,0:T(8,128)S(1)}, u32[]{:S(2)}, u32[]{:S(2)}) collective-permute-start(f32[176,128]{1,0:T(8,128)S(1)} %get-tuple-element.129), channel_id=1, source_target_pairs={{0,1},{1,2},{2,3},{3,0},{4,5},{5,6},{6,7},{7,4},{8,9},{9,10},{10,1... | collective-permute-start | bytes 270344 | tf_op jit(solution)/shard_map/ppermute | solution.py:764
  157.5 7.4 %collective-permute-start.18 = (f32[176,128]{1,0:T(8,128)S(1)}, f32[176,128]{1,0:T(8,128)S(1)}, u32[]{:S(2)}, u32[]{:S(2)}) collective-permute-start(f32[176,128]{1,0:T(8,128)S(1)} %get-tuple-element.128), channel_id=1, source_target_pairs={{0,3},{1,0},{2,1},{3,2},{4,7},{5,4},{6,5},{7,6},{8,11},{9,8},{10,9... | collective-permute-start | bytes 270344 | tf_op jit(solution)/shard_map/ppermute | solution.py:764
  160.1 6.0 %collective-permute-start.16 = (f32[176,128]{1,0:T(8,128)S(1)}, f32[176,128]{1,0:T(8,128)S(1)}, u32[]{:S(2)}, u32[]{:S(2)}) collective-permute-start(f32[176,128]{1,0:T(8,128)S(1)} %get-tuple-element.127), channel_id=1, source_target_pairs={{0,2},{1,3},{2,0},{3,1},{4,6},{5,7},{6,4},{7,5},{8,10},{9,11},{10,... | collective-permute-start | bytes 270344 | tf_op jit(solution)/shard_map/ppermute | solution.py:764
  161.6 8.0 %collective-permute-start.7 = (f32[176,128]{1,0:T(8,128)S(1)}, f32[176,128]{1,0:T(8,128)S(1)}, u32[]{:S(2)}, u32[]{:S(2)}) collective-permute-start(f32[176,128]{1,0:T(8,128)S(1)} %add_add_fusion.8), channel_id=1, source_target_pairs={{0,8},{4,12},{8,16},{12,20},{16,24},{20,28},{24,0},{28,4},{32,40},... | collective-permute-start | bytes 270344 | tf_op jit(solution)/shard_map/ppermute | solution.py:748
  162.8 7.9 %collective-permute-start.8 = (f32[176,128]{1,0:T(8,128)S(1)}, f32[176,128]{1,0:T(8,128)S(1)}, u32[]{:S(2)}, u32[]{:S(2)}) collective-permute-start(f32[176,128]{1,0:T(8,128)S(1)} %add_add_fusion.8), channel_id=1, source_target_pairs={{0,24},{4,28},{8,0},{12,4},{16,8},{20,12},{24,16},{28,20},{32,56},... | collective-permute-start | bytes 270344 | tf_op jit(solution)/shard_map/ppermute | solution.py:748
  164.9 7.4 %collective-permute-start.6 = (f32[176,128]{1,0:T(8,128)S(1)}, f32[176,128]{1,0:T(8,128)S(1)}, u32[]{:S(2)}, u32[]{:S(2)}) collective-permute-start(f32[176,128]{1,0:T(8,128)S(1)} %add_add_fusion.8), channel_id=1, source_target_pairs={{0,16},{4,20},{8,24},{12,28},{16,0},{20,4},{24,8},{28,12},{32,48},... | collective-permute-start | bytes 270344 | tf_op jit(solution)/shard_map/ppermute | solution.py:748
  166.1 7.9 %collective-permute-start.20 = (f32[176,128]{1,0:T(8,128)S(1)}, f32[176,128]{1,0:T(8,128)S(1)}, u32[]{:S(2)}, u32[]{:S(2)}) collective-permute-start(f32[176,128]{1,0:T(8,128)S(1)} %add_add_fusion.5), channel_id=1, source_target_pairs={{0,8},{4,12},{8,16},{12,20},{16,24},{20,28},{24,0},{28,4},{32,40},... | collective-permute-start | bytes 270344 | tf_op jit(solution)/shard_map/ppermute | solution.py:748
  166.2 7.9 %collective-permute-start.21 = (f32[176,128]{1,0:T(8,128)S(1)}, f32[176,128]{1,0:T(8,128)S(1)}, u32[]{:S(2)}, u32[]{:S(2)}) collective-permute-start(f32[176,128]{1,0:T(8,128)S(1)} %add_add_fusion.5), channel_id=1, source_target_pairs={{0,24},{4,28},{8,0},{12,4},{16,8},{20,12},{24,16},{28,20},{32,56},... | collective-permute-start | bytes 270344 | tf_op jit(solution)/shard_map/ppermute | solution.py:748
  169.6 7.8 %collective-permute-start.19 = (f32[176,128]{1,0:T(8,128)S(1)}, f32[176,128]{1,0:T(8,128)S(1)}, u32[]{:S(2)}, u32[]{:S(2)}) collective-permute-start(f32[176,128]{1,0:T(8,128)S(1)} %add_add_fusion.5), channel_id=1, source_target_pairs={{0,16},{4,20},{8,24},{12,28},{16,0},{20,4},{24,8},{28,12},{32,48},... | collective-permute-start | bytes 270344 | tf_op jit(solution)/shard_map/ppermute | solution.py:748
  170.8 21.8 %collective-permute-start.30 = (f32[256,128]{1,0:T(8,128)S(1)}, f32[256,128]{1,0:T(8,128)S(1)}, u32[]{:S(2)}, u32[]{:S(2)}) collective-permute-start(f32[256,128]{1,0:T(8,128)S(1)} %get-tuple-element.126), channel_id=1, source_target_pairs={{0,1},{1,2},{2,3},{3,0},{4,5},{5,6},{6,7},{7,4},{8,9},{9,10},{10,1... | collective-permute-start | bytes 393224 | tf_op jit(solution)/shard_map/ppermute | solution.py:764
  172.3 22.2 %collective-permute-start.31 = (f32[256,128]{1,0:T(8,128)S(1)}, f32[256,128]{1,0:T(8,128)S(1)}, u32[]{:S(2)}, u32[]{:S(2)}) collective-permute-start(f32[256,128]{1,0:T(8,128)S(1)} %get-tuple-element.125), channel_id=1, source_target_pairs={{0,3},{1,0},{2,1},{3,2},{4,7},{5,4},{6,5},{7,6},{8,11},{9,8},{10,9... | collective-permute-start | bytes 393224 | tf_op jit(solution)/shard_map/ppermute | solution.py:764
  174.0 6.6 %collective-permute-start.10 = (f32[176,128]{1,0:T(8,128)S(1)}, f32[176,128]{1,0:T(8,128)S(1)}, u32[]{:S(2)}, u32[]{:S(2)}) collective-permute-start(f32[176,128]{1,0:T(8,128)S(1)} %add_add_fusion.7), channel_id=1, source_target_pairs={{0,32},{4,36},{8,40},{12,44},{16,48},{20,52},{24,56},{28,60},{32,6... | collective-permute-start | bytes 270344 | tf_op jit(solution)/shard_map/ppermute | solution.py:748
  174.1 7.6 %collective-permute-start.11 = (f32[176,128]{1,0:T(8,128)S(1)}, f32[176,128]{1,0:T(8,128)S(1)}, u32[]{:S(2)}, u32[]{:S(2)}) collective-permute-start(f32[176,128]{1,0:T(8,128)S(1)} %add_add_fusion.7), channel_id=1, source_target_pairs={{0,96},{4,100},{8,104},{12,108},{16,112},{20,116},{24,120},{28,124... | collective-permute-start | bytes 270344 | tf_op jit(solution)/shard_map/ppermute | solution.py:748
  177.4 8.2 %collective-permute-start.9 = (f32[176,128]{1,0:T(8,128)S(1)}, f32[176,128]{1,0:T(8,128)S(1)}, u32[]{:S(2)}, u32[]{:S(2)}) collective-permute-start(f32[176,128]{1,0:T(8,128)S(1)} %add_add_fusion.7), channel_id=1, source_target_pairs={{0,64},{4,68},{8,72},{12,76},{16,80},{20,84},{24,88},{28,92},{32,9... | collective-permute-start | bytes 270344 | tf_op jit(solution)/shard_map/ppermute | solution.py:748
  180.7 5.7 %collective-permute-start.23 = (f32[176,128]{1,0:T(8,128)S(1)}, f32[176,128]{1,0:T(8,128)S(1)}, u32[]{:S(2)}, u32[]{:S(2)}) collective-permute-start(f32[176,128]{1,0:T(8,128)S(1)} %add_add_fusion.4), channel_id=1, source_target_pairs={{0,32},{4,36},{8,40},{12,44},{16,48},{20,52},{24,56},{28,60},{32,6... | collective-permute-start | bytes 270344 | tf_op jit(solution)/shard_map/ppermute | solution.py:748
  181.7 6.9 %collective-permute-start.24 = (f32[176,128]{1,0:T(8,128)S(1)}, f32[176,128]{1,0:T(8,128)S(1)}, u32[]{:S(2)}, u32[]{:S(2)}) collective-permute-start(f32[176,128]{1,0:T(8,128)S(1)} %add_add_fusion.4), channel_id=1, source_target_pairs={{0,96},{4,100},{8,104},{12,108},{16,112},{20,116},{24,120},{28,124... | collective-permute-start | bytes 270344 | tf_op jit(solution)/shard_map/ppermute | solution.py:748
  185.6 6.0 %collective-permute-start.22 = (f32[176,128]{1,0:T(8,128)S(1)}, f32[176,128]{1,0:T(8,128)S(1)}, u32[]{:S(2)}, u32[]{:S(2)}) collective-permute-start(f32[176,128]{1,0:T(8,128)S(1)} %add_add_fusion.4), channel_id=1, source_target_pairs={{0,64},{4,68},{8,72},{12,76},{16,80},{20,84},{24,88},{28,92},{32,9... | collective-permute-start | bytes 270344 | tf_op jit(solution)/shard_map/ppermute | solution.py:748
  186.4 8.1 %collective-permute-start.29 = (f32[256,128]{1,0:T(8,128)S(1)}, f32[256,128]{1,0:T(8,128)S(1)}, u32[]{:S(2)}, u32[]{:S(2)}) collective-permute-start(f32[256,128]{1,0:T(8,128)S(1)} %get-tuple-element.124), channel_id=1, source_target_pairs={{0,2},{1,3},{2,0},{3,1},{4,6},{5,7},{6,4},{7,5},{8,10},{9,11},{10,... | collective-permute-start | bytes 393224 | tf_op jit(solution)/shard_map/ppermute | solution.py:764
  188.6 9.2 %collective-permute-start.12 = (f32[176,128]{1,0:T(8,128)S(1)}, f32[176,128]{1,0:T(8,128)S(1)}, u32[]{:S(2)}, u32[]{:S(2)}) collective-permute-start(f32[176,128]{1,0:T(8,128)S(1)} %get-tuple-element.119), channel_id=1, source_target_pairs={{0,1},{1,2},{2,3},{3,0},{4,5},{5,6},{6,7},{7,4},{8,9},{9,10},{10,1... | collective-permute-start | bytes 270344 | tf_op jit(solution)/shard_map/ppermute | solution.py:776
  191.6 7.0 %collective-permute-start.13 = (f32[176,128]{1,0:T(8,128)S(1)}, f32[176,128]{1,0:T(8,128)S(1)}, u32[]{:S(2)}, u32[]{:S(2)}) collective-permute-start(f32[176,128]{1,0:T(8,128)S(1)} %get-tuple-element.119), channel_id=1, source_target_pairs={{0,2},{1,3},{2,0},{3,1},{4,6},{5,7},{6,4},{7,5},{8,10},{9,11},{10,... | collective-permute-start | bytes 270344 | tf_op jit(solution)/shard_map/ppermute | solution.py:776
  192.6 15.3 %collective-permute-start.14 = (f32[176,128]{1,0:T(8,128)S(1)}, f32[176,128]{1,0:T(8,128)S(1)}, u32[]{:S(2)}, u32[]{:S(2)}) collective-permute-start(f32[176,128]{1,0:T(8,128)S(1)} %get-tuple-element.119), channel_id=1, source_target_pairs={{0,3},{1,0},{2,1},{3,2},{4,7},{5,4},{6,5},{7,6},{8,11},{9,8},{10,9... | collective-permute-start | bytes 270344 | tf_op jit(solution)/shard_map/ppermute | solution.py:776
  194.5 6.2 %collective-permute-start.33 = (f32[256,128]{1,0:T(8,128)S(1)}, f32[256,128]{1,0:T(8,128)S(1)}, u32[]{:S(2)}, u32[]{:S(2)}) collective-permute-start(f32[256,128]{1,0:T(8,128)S(1)} %add_add_fusion.2), channel_id=1, source_target_pairs={{0,8},{4,12},{8,16},{12,20},{16,24},{20,28},{24,0},{28,4},{32,40},... | collective-permute-start | bytes 393224 | tf_op jit(solution)/shard_map/ppermute | solution.py:748
  194.6 7.5 %collective-permute-start.34 = (f32[256,128]{1,0:T(8,128)S(1)}, f32[256,128]{1,0:T(8,128)S(1)}, u32[]{:S(2)}, u32[]{:S(2)}) collective-permute-start(f32[256,128]{1,0:T(8,128)S(1)} %add_add_fusion.2), channel_id=1, source_target_pairs={{0,24},{4,28},{8,0},{12,4},{16,8},{20,12},{24,16},{28,20},{32,56},... | collective-permute-start | bytes 393224 | tf_op jit(solution)/shard_map/ppermute | solution.py:748
  197.8 6.5 %collective-permute-start.32 = (f32[256,128]{1,0:T(8,128)S(1)}, f32[256,128]{1,0:T(8,128)S(1)}, u32[]{:S(2)}, u32[]{:S(2)}) collective-permute-start(f32[256,128]{1,0:T(8,128)S(1)} %add_add_fusion.2), channel_id=1, source_target_pairs={{0,16},{4,20},{8,24},{12,28},{16,0},{20,4},{24,8},{28,12},{32,48},... | collective-permute-start | bytes 393224 | tf_op jit(solution)/shard_map/ppermute | solution.py:748
  198.7 10.2 %collective-permute-start.25 = (f32[176,128]{1,0:T(8,128)S(1)}, f32[176,128]{1,0:T(8,128)S(1)}, u32[]{:S(2)}, u32[]{:S(2)}) collective-permute-start(f32[176,128]{1,0:T(8,128)S(1)} %get-tuple-element.117), channel_id=1, source_target_pairs={{0,1},{1,2},{2,3},{3,0},{4,5},{5,6},{6,7},{7,4},{8,9},{9,10},{10,1... | collective-permute-start | bytes 270344 | tf_op jit(solution)/shard_map/ppermute | solution.py:776
  200.8 14.0 %collective-permute-start.26 = (f32[176,128]{1,0:T(8,128)S(1)}, f32[176,128]{1,0:T(8,128)S(1)}, u32[]{:S(2)}, u32[]{:S(2)}) collective-permute-start(f32[176,128]{1,0:T(8,128)S(1)} %get-tuple-element.117), channel_id=1, source_target_pairs={{0,2},{1,3},{2,0},{3,1},{4,6},{5,7},{6,4},{7,5},{8,10},{9,11},{10,... | collective-permute-start | bytes 270344 | tf_op jit(solution)/shard_map/ppermute | solution.py:776
  204.3 6.5 %collective-permute-start.36 = (f32[256,128]{1,0:T(8,128)S(1)}, f32[256,128]{1,0:T(8,128)S(1)}, u32[]{:S(2)}, u32[]{:S(2)}) collective-permute-start(f32[256,128]{1,0:T(8,128)S(1)} %add_add_fusion.1), channel_id=1, source_target_pairs={{0,32},{4,36},{8,40},{12,44},{16,48},{20,52},{24,56},{28,60},{32,6... | collective-permute-start | bytes 393224 | tf_op jit(solution)/shard_map/ppermute | solution.py:748
  204.7 6.2 %collective-permute-start.37 = (f32[256,128]{1,0:T(8,128)S(1)}, f32[256,128]{1,0:T(8,128)S(1)}, u32[]{:S(2)}, u32[]{:S(2)}) collective-permute-start(f32[256,128]{1,0:T(8,128)S(1)} %add_add_fusion.1), channel_id=1, source_target_pairs={{0,96},{4,100},{8,104},{12,108},{16,112},{20,116},{24,120},{28,124... | collective-permute-start | bytes 393224 | tf_op jit(solution)/shard_map/ppermute | solution.py:748
  207.9 6.5 %collective-permute-start.35 = (f32[256,128]{1,0:T(8,128)S(1)}, f32[256,128]{1,0:T(8,128)S(1)}, u32[]{:S(2)}, u32[]{:S(2)}) collective-permute-start(f32[256,128]{1,0:T(8,128)S(1)} %add_add_fusion.1), channel_id=1, source_target_pairs={{0,64},{4,68},{8,72},{12,76},{16,80},{20,84},{24,88},{28,92},{32,9... | collective-permute-start | bytes 393224 | tf_op jit(solution)/shard_map/ppermute | solution.py:748
  208.8 14.3 %copy-start.2 = (f32[704,128]{1,0:T(8,128)}, f32[704,128]{1,0:T(8,128)S(1)}, u32[]{:S(2)}) copy-start(f32[704,128]{1,0:T(8,128)S(1)} %constant_dynamic-update-slice_fusion.8.enc) | copy-start | bytes 1081348
  208.8 8.6 %collective-permute-start.27 = (f32[176,128]{1,0:T(8,128)S(1)}, f32[176,128]{1,0:T(8,128)S(1)}, u32[]{:S(2)}, u32[]{:S(2)}) collective-permute-start(f32[176,128]{1,0:T(8,128)S(1)} %get-tuple-element.117), channel_id=1, source_target_pairs={{0,3},{1,0},{2,1},{3,2},{4,7},{5,4},{6,5},{7,6},{8,11},{9,8},{10,9... | collective-permute-start | bytes 270344 | tf_op jit(solution)/shard_map/ppermute | solution.py:776
  214.5 7.7 %collective-permute-start.38 = (f32[256,128]{1,0:T(8,128)S(1)}, f32[256,128]{1,0:T(8,128)S(1)}, u32[]{:S(2)}, u32[]{:S(2)}) collective-permute-start(f32[256,128]{1,0:T(8,128)S(1)} %get-tuple-element.115), channel_id=1, source_target_pairs={{0,1},{1,2},{2,3},{3,0},{4,5},{5,6},{6,7},{7,4},{8,9},{9,10},{10,1... | collective-permute-start | bytes 393224 | tf_op jit(solution)/shard_map/ppermute | solution.py:776
  214.8 7.4 %collective-permute-start.39 = (f32[256,128]{1,0:T(8,128)S(1)}, f32[256,128]{1,0:T(8,128)S(1)}, u32[]{:S(2)}, u32[]{:S(2)}) collective-permute-start(f32[256,128]{1,0:T(8,128)S(1)} %get-tuple-element.115), channel_id=1, source_target_pairs={{0,2},{1,3},{2,0},{3,1},{4,6},{5,7},{6,4},{7,5},{8,10},{9,11},{10,... | collective-permute-start | bytes 393224 | tf_op jit(solution)/shard_map/ppermute | solution.py:776
  217.5 5.6 %copy-start.1 = (f32[704,128]{1,0:T(8,128)}, f32[704,128]{1,0:T(8,128)S(1)}, u32[]{:S(2)}) copy-start(f32[704,128]{1,0:T(8,128)S(1)} %constant_dynamic-update-slice_fusion.4.dec) | copy-start | bytes 1081348
  217.5 5.6 %collective-permute-start.40 = (f32[256,128]{1,0:T(8,128)S(1)}, f32[256,128]{1,0:T(8,128)S(1)}, u32[]{:S(2)}, u32[]{:S(2)}) collective-permute-start(f32[256,128]{1,0:T(8,128)S(1)} %get-tuple-element.115), channel_id=1, source_target_pairs={{0,3},{1,0},{2,1},{3,2},{4,7},{5,4},{6,5},{7,6},{8,11},{9,8},{10,9... | collective-permute-start | bytes 393224 | tf_op jit(solution)/shard_map/ppermute | solution.py:776
  223.1 0.8 copy-start
